TPU v7x, 128 devices: a whole 4x4x4 slice. The times are simulated.
128 devices in a mesh: row: 8 (over y, x_hi), col: 16 (over x_lo, z, core).
Axes of the slice: x: 4 (x_hi: 2, x_lo: 2; x = x_hi * 2 + x_lo), y: 4, z: 4, core: 2. Of those that a mesh axis runs over, the one named last changes fastest.
Arguments:
- a_blocks: float32 [8, 16, 4, 128, 128], P('row', 'col'), may hold values from -1.2 to 1.2
- a_index: int32 [8, 16, 4], P('row', 'col'), may hold values from -1 to 63, as said below
- b_blocks: float32 [8, 16, 2, 8, 128, 128], P('row', 'col'), may hold values from -1.2 to 1.2
- b_index: int32 [8, 16, 2, 8], P('row', 'col'), may hold values from -1 to 63, as said below
- c_index: int32 [8, 16, 16], P('row', 'col'), may hold values from -1 to 63, as said below
Outputs:
- c_blocks: float32 [8, 16, 16, 128, 128], P('row', 'col')
Inputs may be any that keep to these rules, and one draw needn't show every extreme that they name: `a_index`: within each tile the non-negative entries are distinct and come before the entries -1, which mark empty slots; every tile has at least one block and some tile has all 4 slots filled. `b_index`: within each panel of a device the non-negative entries are distinct and come before the entries -1, which mark empty slots; every panel has at least one block and some panel has all 8 slots filled. `c_index`: within each tile the non-negative entries are distinct and come before the entries -1, which mark empty slots; every tile keeps at least one block and some tile has all 16 slots filled.
All inputs are finite; a program needn't handle non-finite values.
Results may differ from a plain program's by a relative error of at most 0.0003.
Values sent between devices are 32-bit elements; how exact they have to be, the bound alone decides.
No kernel may reach another device: no remote copies, remote signals or barrier semaphores. Data moves between devices by JAX's collectives and lax.ppermute only.
A program may use at most 192 MiB of HBM per device.

v0:
```python
import functools

import jax
import jax.numpy as jnp
import numpy as np
from jax import lax
from jax.experimental import pallas as pl
from jax.experimental.pallas import tpu as pltpu
from jax.sharding import Mesh
from jax.sharding import PartitionSpec as P

SA = 4
PK = 8
NBD = 8
NEAR = 6
AHEAD_FAR, BEHIND_FAR = 2, 1
COL = ("x_lo", "z", "core")
LIST = 512
AHEAD = 8


def lane_maps(columns, lines_per, rows):
    lane = np.arange(rows * columns)
    r, p = lane // columns, lane % columns
    owner = p // lines_per
    across = owner % 2 != r % 2
    far = (owner // 2 - r // 2) % (rows // 2) == 2
    way = across * 1 + far * 2
    first = (lane % columns == 0)[:, None]
    holder = [
        first & (r[:, None] == owner[None, :]) & (p[None, :] % lines_per == h)
        for h in range(lines_per)
    ]
    consumer = first & (r[:, None] == r[None, :])
    alike = (r[:, None] == r[None, :]) & (way[:, None] == way[None, :])
    earlier = alike & (lane[:, None] < lane[None, :])
    return np.stack([*holder, consumer, alike, earlier]).astype(jnp.bfloat16)


def lane_order(rows, columns):
    lane = np.arange(rows * columns)
    y, xh, xl, z, core = lane >> 5, (lane >> 4) & 1, (lane >> 3) & 1, (lane >> 1) & 3, lane & 1
    place = (((core * 4 + z) * 2 + xh) * 2 + xl) * 4 + y
    return (lane[:, None] == place[None, :]).astype(jnp.bfloat16)


def matmul(a, b):
    return jnp.dot(a.astype(jnp.bfloat16), b, preferred_element_type=jnp.float32)


def lands_at(a_line, b):
    meet = (a_line >= 0) & (b >= 0) & ((a_line & (PK - 1)) == (b >> 3))
    return jnp.where(meet, (a_line >> 3) * NBD + (b & (NBD - 1)), -2)


def needed(a, b, c):
    need = jnp.zeros(b.shape, jnp.bool_)
    for s in range(SA):
        lands = lands_at(a[s : s + 1], b)
        for n in range(c.shape[0]):
            need = need | (lands == c[n : n + 1])
    return need


def lane_facts(shape):
    lane = lax.broadcasted_iota(jnp.int32, shape, 1)
    r, p = lane >> 4, lane & 15
    owner = p >> 1
    far = (((owner >> 1) - (r >> 1)) & 3) == 2
    way = ((owner ^ r) & 1) + jnp.where(far, 2, 0)
    return r, p, owner, way


def code(a_slot, part, at, c_slot):
    return ((a_slot * 16 + part) * 128 + at) * 16 + c_slot


def a_of(word):
    return word >> 15


def part_of(word):
    return (word >> 11) & 15


def at_of(word):
    return (word >> 4) & 127


def c_of(word):
    return word & 15


def fetch_block(part, at, refs, dst, sem):
    for i, ref in enumerate(refs):

        def start(ref=ref):
            pltpu.make_async_copy(ref.at[at], dst, sem).start()

        if len(refs) == 1:
            start()
        else:
            pl.when(part == i)(start)


def positions(spots_ref, order_ref):
    spots = spots_ref[...].astype(jnp.float32).astype(jnp.bfloat16)
    return lax.dot_general(
        spots, order_ref[...], (((0,), (0,)), ((), ())), preferred_element_type=jnp.float32
    )


def pack_kernel(sends, me_ref, spots_ref, order_ref, maps_ref, *rest):
    near, packed, info_ref, sems = rest[:3], rest[3 : 3 + len(sends)], rest[-2], rest[-1]
    row, column = me_ref[0], me_ref[1]
    held = positions(spots_ref, order_ref)
    a = held[:8].astype(jnp.int32)
    turned = pltpu.roll(held[8:40], (128 - column) & 127, 1)
    b = matmul(turned[:8], maps_ref[0]) + matmul(turned[8:16], maps_ref[1])
    b = b.astype(jnp.int32)
    c = matmul(turned[16:32], maps_ref[2]).astype(jnp.int32)
    need = needed(a, b, c)

    r, p, owner, way = lane_facts(b.shape)
    t = lax.broadcasted_iota(jnp.int32, b.shape, 0)
    flags = jnp.where(need, 1.0, 0.0)
    alike = matmul(flags, maps_ref[3])
    upto = alike
    for step in (1, 2, 4):
        upto = upto + jnp.where(t >= step, pltpu.roll(upto, step, 0), 0.0)
    rank = (upto - alike + matmul(flags, maps_ref[4])).astype(jnp.int32)
    order = jnp.where(need, way * 128 + rank, -1)

    steps = ((owner >> 1) - (row >> 1)) & 3
    part = jnp.where(steps == 0, 0, jnp.where(steps == 3, 1, 2))
    word = (part * 16 + (p & 1) * 8 + t).astype(jnp.float32)
    words = []
    for slots, which, first, there in sends:
        for e in range(slots):
            hit = (order == which * 128 + first + e) & (r == there(row))
            words.append(jnp.max(jnp.where(hit, word, -1.0)).astype(jnp.int32))
    places = [(i, e) for i, send in enumerate(sends) for e in range(send[0])]
    for n, (i, e) in enumerate(places):

        @pl.when(words[n] >= 0)
        def _():
            fetch_block(words[n] >> 4, words[n] & 15, near, packed[i].at[e], sems.at[n])

    info_ref[0:8] = a
    info_ref[8:16] = b
    info_ref[16:32] = c
    info_ref[32:40] = order
    for n, (i, e) in enumerate(places):

        @pl.when(words[n] >= 0)
        def _():
            pltpu.make_async_copy(near[0].at[0], packed[i].at[e], sems.at[n]).wait()


def pack(me, spots, order, maps, near, sends):
    size = near[0].shape[-1]
    vmem = pl.BlockSpec(memory_space=pltpu.VMEM)
    return pl.pallas_call(
        functools.partial(pack_kernel, sends),
        in_specs=[pl.BlockSpec(memory_space=pltpu.SMEM), vmem, vmem, vmem]
        + [pl.BlockSpec(memory_space=pl.ANY)] * 3,
        out_specs=[vmem] * (len(sends) + 1),
        scratch_shapes=[pltpu.SemaphoreType.DMA((sum(n for n, *_ in sends),))],
        out_shape=[jax.ShapeDtypeStruct((n, size, size), jnp.float32) for n, *_ in sends]
        + [jax.ShapeDtypeStruct((40, 128), jnp.int32)],
        compiler_params=pltpu.CompilerParams(vmem_limit_bytes=16 << 20),
        name="pack",
    )(me, spots, order, maps, *near)


def overflow_kernel(spots_ref, order_ref, maps_ref, over_ref):
    held = positions(spots_ref, order_ref)
    a = held[:8].astype(jnp.int32)
    turned = [held[8:40]] + [pltpu.roll(held[8:40], 128 - q, 1) for q in range(1, 16)]
    b = matmul(jnp.concatenate([x[:8] for x in turned]), maps_ref[0])
    b = b + matmul(jnp.concatenate([x[8:16] for x in turned]), maps_ref[1])
    b = b.astype(jnp.int32)
    c = matmul(jnp.concatenate([x[16:32] for x in turned]), maps_ref[2]).astype(jnp.int32)
    flags = [
        jnp.where(needed(a, b[q * 8 : q * 8 + 8], c[q * 16 : q * 16 + 16]), 1.0, 0.0)
        for q in range(16)
    ]
    alike = matmul(jnp.concatenate(flags), maps_ref[3])
    most = jnp.sum(alike[:8], axis=0, keepdims=True)
    for q in range(1, 16):
        most = jnp.maximum(most, jnp.sum(alike[q * 8 : q * 8 + 8], axis=0, keepdims=True))
    *_, way = lane_facts(most.shape)
    slots = jnp.where(way == 0, 128, jnp.where(way == 1, NEAR, AHEAD_FAR + BEHIND_FAR))
    over_ref[0] = jnp.max(jnp.where(most > slots.astype(jnp.float32), 1.0, 0.0)).astype(jnp.int32)


def overflow(spots, order, maps):
    vmem = pl.BlockSpec(memory_space=pltpu.VMEM)
    return pl.pallas_call(
        overflow_kernel,
        in_specs=[vmem] * 3,
        out_specs=pl.BlockSpec(memory_space=pltpu.SMEM),
        out_shape=jax.ShapeDtypeStruct((1,), jnp.int32),
        compiler_params=pltpu.CompilerParams(vmem_limit_bytes=16 << 20),
        cost_estimate=pl.CostEstimate(flops=10**9, bytes_accessed=10**5, transcendentals=0),
        name="overflow",
    )(spots, order, maps)


def halves(x):
    high = x.astype(jnp.bfloat16)
    return high, (x - high.astype(jnp.float32)).astype(jnp.bfloat16)


def block_product(a, b):
    a_high, a_low = halves(a)
    b_high, b_low = halves(b)
    dot = functools.partial(jnp.dot, preferred_element_type=jnp.float32)
    return dot(a_high, b_high) + (dot(a_high, b_low) + dot(a_low, b_high))


def extract(entries, list_ref):
    def more(state):
        n, word, left = state
        list_ref[n] = word.astype(jnp.int32)
        left = jnp.where(left == word, -1.0, left)
        return n + 1, jnp.max(left), left

    n, *_ = lax.while_loop(
        lambda state: state[1] >= 0, more, (jnp.int32(0), jnp.max(entries), entries)
    )
    list_ref[LIST] = n


def entries_of(info_ref, row):
    b, c, order = info_ref[8:16], info_ref[16:32], info_ref[32:40]
    r, p, owner, way = lane_facts(b.shape)
    t = lax.broadcasted_iota(jnp.int32, b.shape, 0)
    rank = order & 127
    steps = ((owner >> 1) - (row >> 1)) & 3
    part = jnp.where(steps == 0, 0, jnp.where(steps == 3, 1, 2))
    back = (way >= 2) & (rank >= AHEAD_FAR)
    sent_part = jnp.where(way >= 2, way * 2 - 3, 0) + jnp.where(back, 1, 0)
    sent_at = rank - jnp.where(back, AHEAD_FAR, 0)
    sent = (way > 0) & (rank < jnp.where(way == 1, NEAR, AHEAD_FAR + BEHIND_FAR))
    found = [[], [], []]
    for s in range(SA):
        lands = lands_at(info_ref[s : s + 1], b)
        c_slot = jnp.full(b.shape, -1, jnp.int32)
        for n in range(c.shape[0]):
            c_slot = jnp.where(lands == c[n : n + 1], n, c_slot)
        live = (c_slot >= 0) & (r == row)
        a_slot = p * SA + s
        for found_in, mine, code_of in (
            (found[0], way == 0, code(a_slot, part, (p & 1) * 8 + t, c_slot)),
            (found[1], sent, code(a_slot, sent_part, sent_at, c_slot)),
            (found[2], (way > 0) & ~sent, code(a_slot, 0, p * 8 + t, c_slot)),
        ):
            found_in.append(jnp.where(live & mine, code_of, -1).astype(jnp.float32))
    return [jnp.concatenate(x) for x in found]


def multiply_listed(list_ref, a_ref, b_refs, out_ref, a_buf, b_buf, a_sem, b_sem, meanwhile):
    count = list_ref[LIST]

    def fetch(n):
        slot = n % AHEAD
        word = list_ref[n]
        pltpu.make_async_copy(a_ref.at[a_of(word)], a_buf.at[slot], a_sem.at[slot]).start()
        fetch_block(part_of(word), at_of(word), b_refs, b_buf.at[slot], b_sem.at[slot])

    for n in range(AHEAD):

        @pl.when(n < count)
        def _():
            fetch(n)

    meanwhile()

    def step(n, carry):
        slot = n % AHEAD
        pltpu.make_async_copy(a_ref.at[0], a_buf.at[slot], a_sem.at[slot]).wait()
        pltpu.make_async_copy(b_refs[0].at[0], b_buf.at[slot], b_sem.at[slot]).wait()
        out_ref[c_of(list_ref[n])] += block_product(a_buf[slot], b_buf[slot])

        @pl.when(n + AHEAD < count)
        def _():
            fetch(n + AHEAD)

        return carry

    lax.fori_loop(0, count, step, 0)


def own_kernel(me_ref, info_ref, a_ref, *rest):
    b_refs, (out_ref, sent_list, own_list, *buffers) = rest[:3], rest[3:]
    here, sent, _ = entries_of(info_ref, me_ref[0])
    extract(here, own_list)

    def meanwhile():
        extract(sent, sent_list)
        out_ref[...] = jnp.zeros_like(out_ref)

    multiply_listed(own_list, a_ref, b_refs, out_ref, *buffers, meanwhile)


def sent_kernel(list_ref, a_ref, *rest):
    b_refs, (total_ref, out_ref, *buffers) = rest[:-6], rest[-6:]

    def meanwhile():
        out_ref[...] = total_ref[...]

    multiply_listed(list_ref, a_ref, b_refs, out_ref, *buffers, meanwhile)


def rest_kernel(me_ref, info_ref, a_ref, b_ref, total_ref, out_ref, rest_list, *buffers):
    extract(entries_of(info_ref, me_ref[0])[2], rest_list)

    def meanwhile():
        out_ref[...] = total_ref[...]

    multiply_listed(rest_list, a_ref, [b_ref], out_ref, *buffers, meanwhile)


def products(kernel, leading, a_all, b_parts, total, slots, lists_out=False, lists=True):
    size = a_all.shape[-1]
    smem = pl.BlockSpec(memory_space=pltpu.SMEM)
    vmem = pl.BlockSpec(memory_space=pltpu.VMEM)
    operands = [*leading, a_all, *b_parts] + ([] if total is None else [total])
    out = jax.ShapeDtypeStruct((slots, size, size), jnp.float32)
    listing = (LIST + 1,)
    return pl.pallas_call(
        kernel,
        in_specs=[smem if x.ndim == 1 else vmem for x in leading]
        + [pl.BlockSpec(memory_space=pl.ANY)] * (1 + len(b_parts))
        + ([] if total is None else [vmem]),
        out_specs=[vmem, smem] if lists_out else vmem,
        out_shape=[out, jax.ShapeDtypeStruct(listing, jnp.int32)] if lists_out else out,
        scratch_shapes=([pltpu.SMEM(listing, jnp.int32)] if lists else [])
        + [
            pltpu.VMEM((AHEAD, size, size), jnp.float32),
            pltpu.VMEM((AHEAD, size, size), jnp.float32),
            pltpu.SemaphoreType.DMA((AHEAD,)),
            pltpu.SemaphoreType.DMA((AHEAD,)),
        ],
        input_output_aliases={} if total is None else {len(operands) - 1: 0},
        compiler_params=pltpu.CompilerParams(vmem_limit_bytes=16 << 20),
        cost_estimate=pl.CostEstimate(
            flops=8 * 3 * 2 * size**3, bytes_accessed=24 * size * size * 4, transcendentals=0
        ),
        name="products",
    )(*operands)


def to_row(block, rows, there):
    return lax.ppermute(block, "row", [(i, there(i)) for i in range(rows)])


def everywhere(mine, rows, columns):
    axes = ("row", *COL)
    me = lax.axis_index("row") * columns + lax.axis_index(COL)
    held = mine
    for bits in ((5, 6), (3, 4), (1, 2), (0,)):
        group = jnp.zeros((2 ** len(bits),) + held.shape, held.dtype)
        for move in range(2 ** len(bits)):
            flip = sum(((move >> n) & 1) << bit for n, bit in enumerate(bits))
            got = held
            if move:
                got = lax.ppermute(held, axes, [(i ^ flip, i) for i in range(rows * columns)])
            spot = sum((((me ^ flip) >> bit) & 1) << n for n, bit in enumerate(bits))
            group = lax.dynamic_update_index_in_dim(group, got, spot, 0)
        held = group
    return held.reshape(rows * columns, mine.shape[0])


def per_device(a_blocks, a_index, b_blocks, b_index, c_index):
    rows = lax.axis_size("row")
    columns = lax.axis_size(COL)
    row = lax.axis_index("row")
    me = jnp.stack([row, lax.axis_index(COL)])
    hold = columns // rows
    sa, sb, sc = a_blocks.shape[2], b_blocks.shape[3], c_index.shape[2]
    held = hold * sb
    size = a_blocks.shape[-1]

    a_all = lax.all_gather(a_blocks[0, 0], COL).reshape(columns * sa, size, size)

    own = b_blocks[0, 0].reshape(held, size, size)
    behind = to_row(own, rows, lambda i: (i + 2) % rows)
    ahead = to_row(own, rows, lambda i: (i - 2) % rows)
    near = [own, behind, ahead]

    blank = jnp.full((8 - sa,), -1, jnp.int32)
    mine = jnp.concatenate([a_index[0, 0], blank, b_index[0, 0].reshape(-1), c_index[0, 0]])
    spots = everywhere(jnp.pad(mine, (0, 128 - mine.shape[0])), rows, columns)

    order = jnp.asarray(lane_order(rows, columns))
    maps = jnp.asarray(lane_maps(columns, hold, rows))

    sends = [
        (NEAR, 1, 0, lambda i: i ^ 1),
        (AHEAD_FAR, 2, 0, lambda i: (i + 2) & 7),
        (BEHIND_FAR, 2, AHEAD_FAR, lambda i: (i - 2) & 7),
        (AHEAD_FAR, 3, 0, lambda i: ((i + 2) & 7) ^ 1),
        (BEHIND_FAR, 3, AHEAD_FAR, lambda i: ((i - 2) & 7) ^ 1),
    ]
    *packed, info = pack(me, spots, order, maps, near, sends)
    arrived = [to_row(block, rows, there) for block, (*_, there) in zip(packed, sends)]

    total, sent_list = products(own_kernel, [me, info], a_all, near, None, sc, lists_out=True)
    total = products(sent_kernel, [sent_list], a_all, arrived, total, sc, lists=False)

    trips = overflow(spots, order, maps)[0]

    def trip(state):
        done, total = state
        whole = lax.all_gather(own, "row").reshape(rows * held, size, size)
        return done + 1, products(rest_kernel, [me, info], a_all, [whole], total, sc)

    _, total = lax.while_loop(lambda state: state[0] < trips, trip, (jnp.int32(0), total))
    return total[None, None]


def solution(mesh):
    rows, columns = mesh.devices.shape
    mesh = Mesh(mesh.devices.reshape(rows, 2, columns // 4, 2), ("row", *COL))
    in_specs = (
        P("row", COL, None, None, None),
        P("row", COL, None),
        P("row", COL, None, None, None, None),
        P("row", COL, None, None),
        P("row", COL, None),
    )
    out_specs = P("row", COL, None, None, None)
    return jax.shard_map(
        per_device, mesh=mesh, in_specs=in_specs, out_specs=out_specs, check_vma=False
    )
```

profile of v0, /device:TPU:1, one launch (start us, length us, event | category | flops | bytes accessed | tf_op | source)
XLA Modules:
  0.0 70.8 jit_solution(2050726045237759690)
XLA Ops:
  6.5 0.0 all-gather.4.cloned.1.call-start
  6.5 0.7 %all-gather.4.cloned.1.call-update = ((f32[1,1,4,128,128]{4,3,2,1,0:T(8,128)}), f32[16,1,4,128,128]{4,3,2,1,0:T(8,128)}) async-update(((), (), s32[]{:S(2)}) %all-gather.4.cloned.1.call-start, f32[1,1,4,128,128]{4,3,2,1,0:T(8,128)} %param.9) | async-update | bytes 4718616
  7.3 0.8 %reshape_squeeze.6 = s32[16]{0:T(128)S(1)} reshape(s32[1,1,2,8]{3,2,1,0:T(2,128)} %param.12) | data formatting | bytes 128 | tf_op jit(solution)/shard_map/reshape;squeeze | solution.py:394
  8.0 0.7 %pad_add_fusion.1 = s32[40]{0:T(128)S(1)} fusion(s32[16]{0:T(128)} %bitcast.51, s32[16]{0:T(128)S(1)} %reshape_squeeze.6, s32[4]{0:T(128)S(1)} %broadcast.5, s32[4]{0:T(128)} %bitcast.52), kind=kLoop, calls=%fused_computation.11 | loop fusion | flops 120 | bytes 320 | tf_op jit(solution)/shard_map/concatenate | solution.py:394
  8.8 3.8 %collective-permute-start.1 = (s32[128]{0:T(128)S(1)}, s32[128]{0:T(128)S(1)}, u32[]{:S(2)}, u32[]{:S(2)}) collective-permute-start(s32[128]{0:T(128)S(1)} %get-tuple-element.74), channel_id=1, source_target_pairs={{64,0},{65,1},{66,2},{67,3},{68,4},{69,5},{70,6},{71,7},{72,8},{73... | collective-permute-start | bytes 1544 | tf_op jit(solution)/shard_map/ppermute | solution.py:369
  12.5 0.4 collective-permute-start
  12.9 0.4 collective-permute-start.2
  13.3 2.3 %collective-permute-start.11 = (f32[16,128,128]{2,1,0:T(8,128)}, f32[16,128,128]{2,1,0:T(8,128)S(1)}, u32[]{:S(2)}, u32[]{:S(2)}) collective-permute-start(f32[16,128,128]{2,1,0:T(8,128)} %bitcast.46), channel_id=1, source_target_pairs={{0,96},{16,112},{32,0},{48,16},{64,32},{80,48},{96,64},{112,80},{1... | collective-permute-start | bytes 3145736 | tf_op jit(solution)/shard_map/ppermute | solution.py:356
  15.6 0.0 collective-permute-start.10
  15.6 0.1 pad_add_fusion.me_ref
  15.7 0.0 collective-permute-done
  15.8 0.0 collective-permute-done.1
  15.8 0.7 %collective-permute-done.2 = s32[128]{0:T(128)S(1)} collective-permute-done((s32[128]{0:T(128)S(1)}, s32[128]{0:T(128)S(1)}, u32[]{:S(2)}, u32[]{:S(2)}) %collective-permute-start.2) | collective-permute-done | bytes 544 | tf_op jit(solution)/shard_map/ppermute | solution.py:369
  16.6 2.5 %collective-permute-start.5 = (s32[4,128]{1,0:T(4,128)S(1)}, s32[4,128]{1,0:T(4,128)S(1)}, u32[]{:S(2)}, u32[]{:S(2)}) collective-permute-start(s32[4,128]{1,0:T(4,128)S(1)} %dynamic_update_slice.49), channel_id=1, source_target_pairs={{24,0},{25,1},{26,2},{27,3},{28,4},{29,5},{30,6},{31,7},{16,8},{17... | collective-permute-start | bytes 6152 | tf_op jit(solution)/shard_map/ppermute | solution.py:369
  19.1 0.5 collective-permute-start.4
  19.6 0.3 collective-permute-start.3
  19.9 2.5 %collective-permute-done.3 = s32[4,128]{1,0:T(4,128)S(1)} collective-permute-done((s32[4,128]{1,0:T(4,128)S(1)}, s32[4,128]{1,0:T(4,128)S(1)}, u32[]{:S(2)}, u32[]{:S(2)}) %collective-permute-start.3) | collective-permute-done | bytes 2080 | tf_op jit(solution)/shard_map/ppermute | solution.py:369
  22.4 0.7 collective-permute-done.4
  23.1 0.0 collective-permute-done.5
  23.1 3.8 %collective-permute-start.8 = (s32[4,4,128]{2,1,0:T(4,128)S(1)}, s32[4,4,128]{2,1,0:T(4,128)S(1)}, u32[]{:S(2)}, u32[]{:S(2)}) collective-permute-start(s32[4,4,128]{2,1,0:T(4,128)S(1)} %constant_dynamic-update-slice_fusion), channel_id=1, source_target_pairs={{6,0},{7,1},{4,2},{5,3},{2,4},{3,5},{0,6},{1,7},{14,8},{15,9},{12,... | collective-permute-start | bytes 24584 | tf_op jit(solution)/shard_map/ppermute | solution.py:369
  26.9 0.0 collective-permute-start.7
  26.9 0.7 collective-permute-start.6
  27.6 2.2 %collective-permute-done.6 = s32[4,4,128]{2,1,0:T(4,128)S(1)} collective-permute-done((s32[4,4,128]{2,1,0:T(4,128)S(1)}, s32[4,4,128]{2,1,0:T(4,128)S(1)}, u32[]{:S(2)}, u32[]{:S(2)}) %collective-permute-start.6) | collective-permute-done | bytes 8224 | tf_op jit(solution)/shard_map/ppermute | solution.py:369
  29.8 1.1 %collective-permute-done.7 = s32[4,4,128]{2,1,0:T(4,128)S(1)} collective-permute-done((s32[4,4,128]{2,1,0:T(4,128)S(1)}, s32[4,4,128]{2,1,0:T(4,128)S(1)}, u32[]{:S(2)}, u32[]{:S(2)}) %collective-permute-start.7) | collective-permute-done | bytes 8224 | tf_op jit(solution)/shard_map/ppermute | solution.py:369
  30.9 0.0 collective-permute-done.8
  30.9 5.3 %collective-permute-start.9 = (s32[4,4,4,128]{3,2,1,0:T(4,128)S(1)}, s32[4,4,4,128]{3,2,1,0:T(4,128)S(1)}, u32[]{:S(2)}, u32[]{:S(2)}) collective-permute-start(s32[4,4,4,128]{3,2,1,0:T(4,128)S(1)} %bitcast_dynamic-update-slice_fusion.2), channel_id=1, source_target_pairs={{1,0},{0,1},{3,2},{2,3},{5,4},{4,5},{7,6},{6,7},{9,8},{8,9},{11,10... | collective-permute-start | bytes 98312 | tf_op jit(solution)/shard_map/ppermute | solution.py:369
  36.3 0.8 %collective-permute-done.9 = s32[4,4,4,128]{3,2,1,0:T(4,128)S(1)} collective-permute-done((s32[4,4,4,128]{3,2,1,0:T(4,128)S(1)}, s32[4,4,4,128]{3,2,1,0:T(4,128)S(1)}, u32[]{:S(2)}, u32[]{:S(2)}) %collective-permute-start.9) | collective-permute-done | bytes 32800 | tf_op jit(solution)/shard_map/ppermute | solution.py:369
  37.1 0.0 collective-permute-done.11.rest_2_
  37.1 2.7 %collective-permute-done.10.rest_1_ = f32[16,128,128]{2,1,0:T(8,128)S(1)} collective-permute-done((f32[16,128,128]{2,1,0:T(8,128)}, f32[16,128,128]{2,1,0:T(8,128)S(1)}, u32[]{:S(2)}, u32[]{:S(2)}) %collective-permute-start.10) | collective-permute-done | bytes 1048608 | tf_op jit(solution)/shard_map/ppermute | solution.py:356
  39.9 0.0 copy-start.1
  39.9 0.9 %copy-done.1 = bf16[5,128,128]{2,1,0:T(8,128)(2,1)S(1)} copy-done((bf16[5,128,128]{2,1,0:T(8,128)(2,1)S(1)}, bf16[5,128,128]{2,1,0:T(8,128)(2,1)}, u32[]{:S(2)}) %copy-start.1) | copy-done | bytes 163864
  40.8 0.0 copy-start.2
  40.8 0.8 %copy-done.2 = bf16[128,128]{1,0:T(8,128)(2,1)S(1)} copy-done((bf16[128,128]{1,0:T(8,128)(2,1)S(1)}, bf16[128,128]{1,0:T(8,128)(2,1)}, u32[]{:S(2)}) %copy-start.2) | copy-done | bytes 32792
  41.6 2.9 %pack.1 = (f32[6,128,128]{2,1,0:T(8,128)S(1)}, f32[2,128,128]{2,1,0:T(8,128)S(1)}, f32[1,128,128]{2,1,0:T(8,128)}, f32[2,128,128]{2,1,0:T(8,128)S(1)}, f32[1,128,128]{2,1,0:T(8,128)}, /*index=5*/s32[40,128]{1,0:T(8,128)}) custom-call(s32[2]{0:T(128)S(1)} %pad_add_fusion.me_ref, s32[128,128]{1,0:T(8,128)S(1)} %bitcast.41, bf16[128,128]{1,0:T(8,128)(2,1)S(1)} %copy-done.2, ...), custom_call_target="tpu_custom_call" | custom-call | tf_op jit(solution)/shard_map/pack/pallas_call | solution.py:163
  44.5 2.7 %collective-permute-start.12 = (f32[6,128,128]{2,1,0:T(8,128)S(1)}, f32[6,128,128]{2,1,0:T(8,128)S(1)}, u32[]{:S(2)}, u32[]{:S(2)}) collective-permute-start(f32[6,128,128]{2,1,0:T(8,128)S(1)} %get-tuple-element.53), channel_id=1, source_target_pairs={{0,16},{16,0},{32,48},{48,32},{64,80},{80,64},{96,112},{112,96},{1... | collective-permute-start | bytes 1179656 | tf_op jit(solution)/shard_map/ppermute | solution.py:356
  47.2 0.0 collective-permute-start.13
  47.2 0.0 collective-permute-start.15
  47.2 2.7 %collective-permute-start.14 = (f32[1,128,128]{2,1,0:T(8,128)}, f32[1,128,128]{2,1,0:T(8,128)S(1)}, u32[]{:S(2)}, u32[]{:S(2)}) collective-permute-start(f32[1,128,128]{2,1,0:T(8,128)} %get-tuple-element.55), channel_id=1, source_target_pairs={{0,96},{16,112},{32,0},{48,16},{64,32},{80,48},{96,64},{112,80},{1... | collective-permute-start | bytes 196616 | tf_op jit(solution)/shard_map/ppermute | solution.py:356
  49.9 3.8 %collective-permute-start.16 = (f32[1,128,128]{2,1,0:T(8,128)}, f32[1,128,128]{2,1,0:T(8,128)S(1)}, u32[]{:S(2)}, u32[]{:S(2)}) collective-permute-start(f32[1,128,128]{2,1,0:T(8,128)} %get-tuple-element.57), channel_id=1, source_target_pairs={{0,112},{16,96},{32,16},{48,0},{64,48},{80,32},{96,80},{112,64},{1... | collective-permute-start | bytes 196616 | tf_op jit(solution)/shard_map/ppermute | solution.py:356
  53.8 1.7 %overflow.1 = s32[1]{0:T(128)} custom-call(s32[128,128]{1,0:T(8,128)S(1)} %bitcast.42, bf16[128,128]{1,0:T(8,128)(2,1)S(1)} %copy-done.2, bf16[5,128,128]{2,1,0:T(8,128)(2,1)S(1)} %copy-done.1), custom_call_target="tpu_custom_call" | custom-call | flops 1000000000 | bytes 100000 | tf_op jit(solution)/shard_map/overflow/pallas_call | solution.py:199
  55.5 0.0 all-gather.4.cloned.1.call-done
  55.5 0.0 copy-start.3
  55.5 3.1 %products.3 = (f32[16,128,128]{2,1,0:T(8,128)S(1)}, s32[513]{0:T(1024)S(1)}) custom-call(s32[2]{0:T(128)S(1)} %pad_add_fusion.me_ref, s32[40,128]{1,0:T(8,128)} %get-tuple-element.125.info_ref, f32[64,128,128]{2,1,0:T(8,128)} %bitcast.43, f32[16,128,128]{2,1,0:T(8,128)} %bitcast.49, f32[16,128,128]{2,1,0:T(8,128)S(1)} %collective-permute-done.10.rest_1_, ...), custom_call_target="tpu_custom_call" | custom-call | flops 100663296 | bytes 1572864 | tf_op jit(solution)/shard_map/products/pallas_call | solution.py:332
  58.6 0.0 collective-permute-done.14.rest_2_
  58.6 2.0 %collective-permute-done.16.rest_4_ = f32[1,128,128]{2,1,0:T(8,128)S(1)} collective-permute-done((f32[1,128,128]{2,1,0:T(8,128)}, f32[1,128,128]{2,1,0:T(8,128)S(1)}, u32[]{:S(2)}, u32[]{:S(2)}) %collective-permute-start.16) | collective-permute-done | bytes 65568 | tf_op jit(solution)/shard_map/ppermute | solution.py:356
  60.7 0.0 collective-permute-done.13.rest_1_
  60.7 0.0 collective-permute-done.15.rest_3_
  60.7 0.0 collective-permute-done.12.rest_0_
  60.7 0.0 copy-done.3
  60.7 1.6 %products.4 = f32[16,128,128]{2,1,0:T(8,128)S(1)} custom-call(s32[513]{0:T(1024)S(1)} %get-tuple-element.52.list_ref, f32[64,128,128]{2,1,0:T(8,128)S(1)} %bitcast.45, f32[6,128,128]{2,1,0:T(8,128)S(1)} %collective-permute-done.12.rest_0_, f32[2,128,128]{2,1,0:T(8,128)S(1)} %collective-permute-done.13.rest_1_, ...), custom_call_target="tpu_custom_call", output_to_operand_aliasing={{}: (7, {})} | custom-call | flops 100663296 | bytes 1572864 | tf_op jit(solution)/shard_map/products/pallas_call | solution.py:332
  62.4 0.0 copy-start.4
  62.4 1.0 %copy-done.4 = f32[16,128,128]{2,1,0:T(8,128)} copy-done((f32[16,128,128]{2,1,0:T(8,128)}, f32[16,128,128]{2,1,0:T(8,128)S(1)}, u32[]{:S(2)}) %copy-start.4) | copy-done | bytes 1048600
  63.3 0.6 while.10
  (20 shorter events, 0.2 us)
Async XLA Ops:
  6.5 49.0 %all-gather.4.cloned.1.call-start = ((), (), s32[]{:S(2)}) async-start(), calls=%async_computation | async-start | bytes 4456448 | tf_op jit(solution)/shard_map/all_gather | solution.py:386
  8.8 7.0 %collective-permute-start.1 = (s32[128]{0:T(128)S(1)}, s32[128]{0:T(128)S(1)}, u32[]{:S(2)}, u32[]{:S(2)}) collective-permute-start(s32[128]{0:T(128)S(1)} %get-tuple-element.74), channel_id=1, source_target_pairs={{64,0},{65,1},{66,2},{67,3},{68,4},{69,5},{70,6},{71,7},{72,8},{73... | collective-permute-start | bytes 1544 | tf_op jit(solution)/shard_map/ppermute | solution.py:369
  12.5 3.2 %collective-permute-start = (s32[128]{0:T(128)S(1)}, s32[128]{0:T(128)S(1)}, u32[]{:S(2)}, u32[]{:S(2)}) collective-permute-start(s32[128]{0:T(128)S(1)} %get-tuple-element.74), channel_id=1, source_target_pairs={{32,0},{33,1},{34,2},{35,3},{36,4},{37,5},{38,6},{39,7},{40,8},{41... | collective-permute-start | bytes 1544 | tf_op jit(solution)/shard_map/ppermute | solution.py:369
  12.9 3.6 %collective-permute-start.2 = (s32[128]{0:T(128)S(1)}, s32[128]{0:T(128)S(1)}, u32[]{:S(2)}, u32[]{:S(2)}) collective-permute-start(s32[128]{0:T(128)S(1)} %get-tuple-element.74), channel_id=1, source_target_pairs={{96,0},{97,1},{98,2},{99,3},{100,4},{101,5},{102,6},{103,7},{104,8... | collective-permute-start | bytes 1544 | tf_op jit(solution)/shard_map/ppermute | solution.py:369
  13.3 23.8 %collective-permute-start.11 = (f32[16,128,128]{2,1,0:T(8,128)}, f32[16,128,128]{2,1,0:T(8,128)S(1)}, u32[]{:S(2)}, u32[]{:S(2)}) collective-permute-start(f32[16,128,128]{2,1,0:T(8,128)} %bitcast.46), channel_id=1, source_target_pairs={{0,96},{16,112},{32,0},{48,16},{64,32},{80,48},{96,64},{112,80},{1... | collective-permute-start | bytes 3145736 | tf_op jit(solution)/shard_map/ppermute | solution.py:356
  15.6 24.3 %collective-permute-start.10 = (f32[16,128,128]{2,1,0:T(8,128)}, f32[16,128,128]{2,1,0:T(8,128)S(1)}, u32[]{:S(2)}, u32[]{:S(2)}) collective-permute-start(f32[16,128,128]{2,1,0:T(8,128)} %bitcast.47), channel_id=1, source_target_pairs={{0,32},{16,48},{32,64},{48,80},{64,96},{80,112},{96,0},{112,16},{1... | collective-permute-start | bytes 3145736 | tf_op jit(solution)/shard_map/ppermute | solution.py:356
  16.6 6.5 %collective-permute-start.5 = (s32[4,128]{1,0:T(4,128)S(1)}, s32[4,128]{1,0:T(4,128)S(1)}, u32[]{:S(2)}, u32[]{:S(2)}) collective-permute-start(s32[4,128]{1,0:T(4,128)S(1)} %dynamic_update_slice.49), channel_id=1, source_target_pairs={{24,0},{25,1},{26,2},{27,3},{28,4},{29,5},{30,6},{31,7},{16,8},{17... | collective-permute-start | bytes 6152 | tf_op jit(solution)/shard_map/ppermute | solution.py:369
  19.1 3.9 %collective-permute-start.4 = (s32[4,128]{1,0:T(4,128)S(1)}, s32[4,128]{1,0:T(4,128)S(1)}, u32[]{:S(2)}, u32[]{:S(2)}) collective-permute-start(s32[4,128]{1,0:T(4,128)S(1)} %dynamic_update_slice.49), channel_id=1, source_target_pairs={{16,0},{17,1},{18,2},{19,3},{20,4},{21,5},{22,6},{23,7},{24,8},{25... | collective-permute-start | bytes 6152 | tf_op jit(solution)/shard_map/ppermute | solution.py:369
  19.6 2.7 %collective-permute-start.3 = (s32[4,128]{1,0:T(4,128)S(1)}, s32[4,128]{1,0:T(4,128)S(1)}, u32[]{:S(2)}, u32[]{:S(2)}) collective-permute-start(s32[4,128]{1,0:T(4,128)S(1)} %dynamic_update_slice.49), channel_id=1, source_target_pairs={{8,0},{9,1},{10,2},{11,3},{12,4},{13,5},{14,6},{15,7},{0,8},{1,9},... | collective-permute-start | bytes 6152 | tf_op jit(solution)/shard_map/ppermute | solution.py:369
  23.1 7.9 %collective-permute-start.8 = (s32[4,4,128]{2,1,0:T(4,128)S(1)}, s32[4,4,128]{2,1,0:T(4,128)S(1)}, u32[]{:S(2)}, u32[]{:S(2)}) collective-permute-start(s32[4,4,128]{2,1,0:T(4,128)S(1)} %constant_dynamic-update-slice_fusion), channel_id=1, source_target_pairs={{6,0},{7,1},{4,2},{5,3},{2,4},{3,5},{0,6},{1,7},{14,8},{15,9},{12,... | collective-permute-start | bytes 24584 | tf_op jit(solution)/shard_map/ppermute | solution.py:369
  26.9 4.0 %collective-permute-start.7 = (s32[4,4,128]{2,1,0:T(4,128)S(1)}, s32[4,4,128]{2,1,0:T(4,128)S(1)}, u32[]{:S(2)}, u32[]{:S(2)}) collective-permute-start(s32[4,4,128]{2,1,0:T(4,128)S(1)} %constant_dynamic-update-slice_fusion), channel_id=1, source_target_pairs={{4,0},{5,1},{6,2},{7,3},{0,4},{1,5},{2,6},{3,7},{12,8},{13,9},{14,... | collective-permute-start | bytes 24584 | tf_op jit(solution)/shard_map/ppermute | solution.py:369
  26.9 2.9 %collective-permute-start.6 = (s32[4,4,128]{2,1,0:T(4,128)S(1)}, s32[4,4,128]{2,1,0:T(4,128)S(1)}, u32[]{:S(2)}, u32[]{:S(2)}) collective-permute-start(s32[4,4,128]{2,1,0:T(4,128)S(1)} %constant_dynamic-update-slice_fusion), channel_id=1, source_target_pairs={{2,0},{3,1},{0,2},{1,3},{6,4},{7,5},{4,6},{5,7},{10,8},{11,9},{8,1... | collective-permute-start | bytes 24584 | tf_op jit(solution)/shard_map/ppermute | solution.py:369
  30.9 6.2 %collective-permute-start.9 = (s32[4,4,4,128]{3,2,1,0:T(4,128)S(1)}, s32[4,4,4,128]{3,2,1,0:T(4,128)S(1)}, u32[]{:S(2)}, u32[]{:S(2)}) collective-permute-start(s32[4,4,4,128]{3,2,1,0:T(4,128)S(1)} %bitcast_dynamic-update-slice_fusion.2), channel_id=1, source_target_pairs={{1,0},{0,1},{3,2},{2,3},{5,4},{4,5},{7,6},{6,7},{9,8},{8,9},{11,10... | collective-permute-start | bytes 98312 | tf_op jit(solution)/shard_map/ppermute | solution.py:369
  39.9 0.9 %copy-start.1 = (bf16[5,128,128]{2,1,0:T(8,128)(2,1)S(1)}, bf16[5,128,128]{2,1,0:T(8,128)(2,1)}, u32[]{:S(2)}) copy-start(bf16[5,128,128]{2,1,0:T(8,128)(2,1)} %constant.91.clone.maps_ref) | copy-start | bytes 491524
  40.8 0.8 %copy-start.2 = (bf16[128,128]{1,0:T(8,128)(2,1)S(1)}, bf16[128,128]{1,0:T(8,128)(2,1)}, u32[]{:S(2)}) copy-start(bf16[128,128]{1,0:T(8,128)(2,1)} %constant.90.clone.order_ref) | copy-start | bytes 98308
  44.5 16.2 %collective-permute-start.12 = (f32[6,128,128]{2,1,0:T(8,128)S(1)}, f32[6,128,128]{2,1,0:T(8,128)S(1)}, u32[]{:S(2)}, u32[]{:S(2)}) collective-permute-start(f32[6,128,128]{2,1,0:T(8,128)S(1)} %get-tuple-element.53), channel_id=1, source_target_pairs={{0,16},{16,0},{32,48},{48,32},{64,80},{80,64},{96,112},{112,96},{1... | collective-permute-start | bytes 1179656 | tf_op jit(solution)/shard_map/ppermute | solution.py:356
  47.2 13.5 %collective-permute-start.13 = (f32[2,128,128]{2,1,0:T(8,128)S(1)}, f32[2,128,128]{2,1,0:T(8,128)S(1)}, u32[]{:S(2)}, u32[]{:S(2)}) collective-permute-start(f32[2,128,128]{2,1,0:T(8,128)S(1)} %get-tuple-element.54), channel_id=1, source_target_pairs={{0,32},{16,48},{32,64},{48,80},{64,96},{80,112},{96,0},{112,16},{1... | collective-permute-start | bytes 393224 | tf_op jit(solution)/shard_map/ppermute | solution.py:356
  47.2 13.5 %collective-permute-start.15 = (f32[2,128,128]{2,1,0:T(8,128)S(1)}, f32[2,128,128]{2,1,0:T(8,128)S(1)}, u32[]{:S(2)}, u32[]{:S(2)}) collective-permute-start(f32[2,128,128]{2,1,0:T(8,128)S(1)} %get-tuple-element.56), channel_id=1, source_target_pairs={{0,48},{16,32},{32,80},{48,64},{64,112},{80,96},{96,16},{112,0},{1... | collective-permute-start | bytes 393224 | tf_op jit(solution)/shard_map/ppermute | solution.py:356
  47.2 11.4 %collective-permute-start.14 = (f32[1,128,128]{2,1,0:T(8,128)}, f32[1,128,128]{2,1,0:T(8,128)S(1)}, u32[]{:S(2)}, u32[]{:S(2)}) collective-permute-start(f32[1,128,128]{2,1,0:T(8,128)} %get-tuple-element.55), channel_id=1, source_target_pairs={{0,96},{16,112},{32,0},{48,16},{64,32},{80,48},{96,64},{112,80},{1... | collective-permute-start | bytes 196616 | tf_op jit(solution)/shard_map/ppermute | solution.py:356
  49.9 10.7 %collective-permute-start.16 = (f32[1,128,128]{2,1,0:T(8,128)}, f32[1,128,128]{2,1,0:T(8,128)S(1)}, u32[]{:S(2)}, u32[]{:S(2)}) collective-permute-start(f32[1,128,128]{2,1,0:T(8,128)} %get-tuple-element.57), channel_id=1, source_target_pairs={{0,112},{16,96},{32,16},{48,0},{64,48},{80,32},{96,80},{112,64},{1... | collective-permute-start | bytes 196616 | tf_op jit(solution)/shard_map/ppermute | solution.py:356
  55.5 5.2 %copy-start.3 = (f32[16,1,4,128,128]{4,3,2,1,0:T(8,128)S(1)}, f32[16,1,4,128,128]{4,3,2,1,0:T(8,128)}, u32[]{:S(2)}) copy-start(f32[16,1,4,128,128]{4,3,2,1,0:T(8,128)} %all-gather.4.cloned.1.call-done) | copy-start | bytes 12582916
  62.4 1.0 %copy-start.4 = (f32[16,128,128]{2,1,0:T(8,128)}, f32[16,128,128]{2,1,0:T(8,128)S(1)}, u32[]{:S(2)}) copy-start(f32[16,128,128]{2,1,0:T(8,128)S(1)} %products.4) | copy-start | bytes 3145732
Sparse Core Ops, SparseCore 0:
  9.1 41.1 all-gather.3
where the time goes:
time: 71.9 us; the launch traced here: 70.8 us
  starting transfers between devices  29.3 us (41%)
  waiting for transfers between devices  13.6 us (19%)
  between operations  13.5 us (19%)
  Pallas kernels  9.37 us (13%)
  local copies, waits for them, and re-layouts  3.65 us (5%)
  other arithmetic  0.82 us (1%)
    ppermute x10, starting transfers between devices, everywhere(): lax.ppermute(held, axes, [(i ^ flip, i) for i in range(rows * columns)])  17.7 us
    ppermute x7, starting transfers between devices, to_row(): return lax.ppermute(block, 'row', [(i, there(i)) for i in range(rows)])  11.6 us
    ppermute x10, waiting for transfers between devices, everywhere(): lax.ppermute(held, axes, [(i ^ flip, i) for i in range(rows * columns)])  8.03 us
    ppermute x7, waiting for transfers between devices, to_row(): return lax.ppermute(block, 'row', [(i, there(i)) for i in range(rows)])  4.79 us
    pallas_call x2, Pallas kernels, products(): pl.pallas_call(kernel, in_specs=[smem if x.ndim == 1 else vmem for x in l...  4.73 us
    pallas_call x1, Pallas kernels, pack(): pl.pallas_call(functools.partial(pack_kernel, sends), in_specs=[pl.BlockS...  2.91 us
    unnamed x8, local copies, waits for them, and re-layouts  2.64 us
    pallas_call x1, Pallas kernels, overflow(): pl.pallas_call(overflow_kernel, in_specs=[vmem] * 3, out_specs=pl.BlockSp...  1.73 us
  transfers between devices with their start and end apart: 18, of which 8 were waited for; matrix products, arithmetic and copies ran while one was open for 3% of the time, Pallas kernels for 11%

commit v1 on v0

--- a/solution.py
+++ b/solution.py
@@ -2,7 +2,6 @@
 
 import jax
 import jax.numpy as jnp
-import numpy as np
 from jax import lax
 from jax.experimental import pallas as pl
 from jax.experimental.pallas import tpu as pltpu
@@ -13,35 +12,10 @@
 PK = 8
 NBD = 8
 NEAR = 6
-AHEAD_FAR, BEHIND_FAR = 2, 1
+FAR = 3
 COL = ("x_lo", "z", "core")
 LIST = 512
 AHEAD = 8
-
-
-def lane_maps(columns, lines_per, rows):
-    lane = np.arange(rows * columns)
-    r, p = lane // columns, lane % columns
-    owner = p // lines_per
-    across = owner % 2 != r % 2
-    far = (owner // 2 - r // 2) % (rows // 2) == 2
-    way = across * 1 + far * 2
-    first = (lane % columns == 0)[:, None]
-    holder = [
-        first & (r[:, None] == owner[None, :]) & (p[None, :] % lines_per == h)
-        for h in range(lines_per)
-    ]
-    consumer = first & (r[:, None] == r[None, :])
-    alike = (r[:, None] == r[None, :]) & (way[:, None] == way[None, :])
-    earlier = alike & (lane[:, None] < lane[None, :])
-    return np.stack([*holder, consumer, alike, earlier]).astype(jnp.bfloat16)
-
-
-def lane_order(rows, columns):
-    lane = np.arange(rows * columns)
-    y, xh, xl, z, core = lane >> 5, (lane >> 4) & 1, (lane >> 3) & 1, (lane >> 1) & 3, lane & 1
-    place = (((core * 4 + z) * 2 + xh) * 2 + xl) * 4 + y
-    return (lane[:, None] == place[None, :]).astype(jnp.bfloat16)
 
 
 def matmul(a, b):
@@ -62,8 +36,8 @@
     return need
 
 
-def lane_facts(shape):
-    lane = lax.broadcasted_iota(jnp.int32, shape, 1)
+def lane_facts(shape, axis=1):
+    lane = lax.broadcasted_iota(jnp.int32, shape, axis)
     r, p = lane >> 4, lane & 15
     owner = p >> 1
     far = (((owner >> 1) - (r >> 1)) & 3) == 2
@@ -103,17 +77,40 @@
             pl.when(part == i)(start)
 
 
-def positions(spots_ref, order_ref):
+def make_maps(maps_ref):
+    shape = maps_ref.shape[1:]
+    lane = lax.broadcasted_iota(jnp.int32, shape, 1)
+    down = lax.broadcasted_iota(jnp.int32, shape, 0)
+    r, p, owner, way = lane_facts(shape)
+    r_down, p_down, _, way_down = lane_facts(shape, 0)
+    holder = (p_down == 0) & (r_down == owner)
+    alike = (r == r_down) & (way == way_down)
+    y, xh, xl, z, core = lane >> 5, (lane >> 4) & 1, (lane >> 3) & 1, (lane >> 1) & 3, lane & 1
+    listed_at = (((core * 4 + z) * 2 + xh) * 2 + xl) * 4 + y
+    for n, flags in enumerate(
+        [
+            holder & ((p & 1) == 0),
+            holder & ((p & 1) == 1),
+            (p_down == 0) & (r == r_down),
+            alike,
+            alike & (down < lane),
+            down == listed_at,
+        ]
+    ):
+        maps_ref[n] = jnp.where(flags, 1.0, 0.0).astype(jnp.bfloat16)
+
+
+def positions(spots_ref, maps_ref):
     spots = spots_ref[...].astype(jnp.float32).astype(jnp.bfloat16)
     return lax.dot_general(
-        spots, order_ref[...], (((0,), (0,)), ((), ())), preferred_element_type=jnp.float32
+        spots, maps_ref[5], (((0,), (0,)), ((), ())), preferred_element_type=jnp.float32
     )
 
 
-def pack_kernel(sends, me_ref, spots_ref, order_ref, maps_ref, *rest):
-    near, packed, info_ref, sems = rest[:3], rest[3 : 3 + len(sends)], rest[-2], rest[-1]
+def plan_kernel(sends, me_ref, spots_ref, pack_list, own_list, sent_list, info_ref, maps_ref):
     row, column = me_ref[0], me_ref[1]
-    held = positions(spots_ref, order_ref)
+    make_maps(maps_ref)
+    held = positions(spots_ref, maps_ref)
     a = held[:8].astype(jnp.int32)
     turned = pltpu.roll(held[8:40], (128 - column) & 127, 1)
     b = matmul(turned[:8], maps_ref[0]) + matmul(turned[8:16], maps_ref[1])
@@ -134,47 +131,74 @@
     steps = ((owner >> 1) - (row >> 1)) & 3
     part = jnp.where(steps == 0, 0, jnp.where(steps == 3, 1, 2))
     word = (part * 16 + (p & 1) * 8 + t).astype(jnp.float32)
-    words = []
-    for slots, which, first, there in sends:
+    n = 0
+    for slots, which, there in sends:
         for e in range(slots):
-            hit = (order == which * 128 + first + e) & (r == there(row))
-            words.append(jnp.max(jnp.where(hit, word, -1.0)).astype(jnp.int32))
-    places = [(i, e) for i, send in enumerate(sends) for e in range(send[0])]
-    for n, (i, e) in enumerate(places):
-
-        @pl.when(words[n] >= 0)
-        def _():
-            fetch_block(words[n] >> 4, words[n] & 15, near, packed[i].at[e], sems.at[n])
+            hit = (order == which * 128 + e) & (r == there(row))
+            pack_list[n] = jnp.max(jnp.where(hit, word, -1.0)).astype(jnp.int32)
+            n += 1
 
     info_ref[0:8] = a
     info_ref[8:16] = b
     info_ref[16:32] = c
     info_ref[32:40] = order
+    here, sent, _ = entries_of(info_ref, row)
+    extract(here, own_list)
+    extract(sent, sent_list)
+
+
+def plan(me, spots, sends):
+    smem = pl.BlockSpec(memory_space=pltpu.SMEM)
+    vmem = pl.BlockSpec(memory_space=pltpu.VMEM)
+    return pl.pallas_call(
+        functools.partial(plan_kernel, sends),
+        in_specs=[smem, vmem],
+        out_specs=[smem, smem, smem, vmem, vmem],
+        out_shape=[
+            jax.ShapeDtypeStruct((sum(n for n, *_ in sends),), jnp.int32),
+            jax.ShapeDtypeStruct((LIST + 1,), jnp.int32),
+            jax.ShapeDtypeStruct((LIST + 1,), jnp.int32),
+            jax.ShapeDtypeStruct((40, 128), jnp.int32),
+            jax.ShapeDtypeStruct((6, 128, 128), jnp.bfloat16),
+        ],
+        compiler_params=pltpu.CompilerParams(vmem_limit_bytes=16 << 20),
+        name="plan",
+    )(me, spots)
+
+
+def pack_kernel(sizes, list_ref, *rest):
+    near, packed, sems = rest[:3], rest[3:-1], rest[-1]
+    places = [(i, e) for i, size in enumerate(sizes) for e in range(size)]
     for n, (i, e) in enumerate(places):
-
-        @pl.when(words[n] >= 0)
+        word = list_ref[n]
+
+        @pl.when(word >= 0)
+        def _():
+            fetch_block(word >> 4, word & 15, near, packed[i].at[e], sems.at[n])
+
+    for n, (i, e) in enumerate(places):
+
+        @pl.when(list_ref[n] >= 0)
         def _():
             pltpu.make_async_copy(near[0].at[0], packed[i].at[e], sems.at[n]).wait()
 
 
-def pack(me, spots, order, maps, near, sends):
+def pack(listing, near, sizes):
     size = near[0].shape[-1]
-    vmem = pl.BlockSpec(memory_space=pltpu.VMEM)
     return pl.pallas_call(
-        functools.partial(pack_kernel, sends),
-        in_specs=[pl.BlockSpec(memory_space=pltpu.SMEM), vmem, vmem, vmem]
+        functools.partial(pack_kernel, sizes),
+        in_specs=[pl.BlockSpec(memory_space=pltpu.SMEM)]
         + [pl.BlockSpec(memory_space=pl.ANY)] * 3,
-        out_specs=[vmem] * (len(sends) + 1),
-        scratch_shapes=[pltpu.SemaphoreType.DMA((sum(n for n, *_ in sends),))],
-        out_shape=[jax.ShapeDtypeStruct((n, size, size), jnp.float32) for n, *_ in sends]
-        + [jax.ShapeDtypeStruct((40, 128), jnp.int32)],
+        out_specs=[pl.BlockSpec(memory_space=pltpu.VMEM)] * len(sizes),
+        scratch_shapes=[pltpu.SemaphoreType.DMA((sum(sizes),))],
+        out_shape=[jax.ShapeDtypeStruct((n, size, size), jnp.float32) for n in sizes],
         compiler_params=pltpu.CompilerParams(vmem_limit_bytes=16 << 20),
         name="pack",
-    )(me, spots, order, maps, *near)
-
-
-def overflow_kernel(spots_ref, order_ref, maps_ref, over_ref):
-    held = positions(spots_ref, order_ref)
+    )(listing, *near)
+
+
+def overflow_kernel(spots_ref, maps_ref, over_ref):
+    held = positions(spots_ref, maps_ref)
     a = held[:8].astype(jnp.int32)
     turned = [held[8:40]] + [pltpu.roll(held[8:40], 128 - q, 1) for q in range(1, 16)]
     b = matmul(jnp.concatenate([x[:8] for x in turned]), maps_ref[0])
@@ -190,21 +214,21 @@
     for q in range(1, 16):
         most = jnp.maximum(most, jnp.sum(alike[q * 8 : q * 8 + 8], axis=0, keepdims=True))
     *_, way = lane_facts(most.shape)
-    slots = jnp.where(way == 0, 128, jnp.where(way == 1, NEAR, AHEAD_FAR + BEHIND_FAR))
+    slots = jnp.where(way == 0, 128, jnp.where(way == 1, NEAR, FAR))
     over_ref[0] = jnp.max(jnp.where(most > slots.astype(jnp.float32), 1.0, 0.0)).astype(jnp.int32)
 
 
-def overflow(spots, order, maps):
+def overflow(spots, maps):
     vmem = pl.BlockSpec(memory_space=pltpu.VMEM)
     return pl.pallas_call(
         overflow_kernel,
-        in_specs=[vmem] * 3,
+        in_specs=[vmem] * 2,
         out_specs=pl.BlockSpec(memory_space=pltpu.SMEM),
         out_shape=jax.ShapeDtypeStruct((1,), jnp.int32),
         compiler_params=pltpu.CompilerParams(vmem_limit_bytes=16 << 20),
         cost_estimate=pl.CostEstimate(flops=10**9, bytes_accessed=10**5, transcendentals=0),
         name="overflow",
-    )(spots, order, maps)
+    )(spots, maps)
 
 
 def halves(x):
@@ -239,10 +263,7 @@
     rank = order & 127
     steps = ((owner >> 1) - (row >> 1)) & 3
     part = jnp.where(steps == 0, 0, jnp.where(steps == 3, 1, 2))
-    back = (way >= 2) & (rank >= AHEAD_FAR)
-    sent_part = jnp.where(way >= 2, way * 2 - 3, 0) + jnp.where(back, 1, 0)
-    sent_at = rank - jnp.where(back, AHEAD_FAR, 0)
-    sent = (way > 0) & (rank < jnp.where(way == 1, NEAR, AHEAD_FAR + BEHIND_FAR))
+    sent = (way > 0) & (rank < jnp.where(way == 1, NEAR, FAR))
     found = [[], [], []]
     for s in range(SA):
         lands = lands_at(info_ref[s : s + 1], b)
@@ -253,7 +274,7 @@
         a_slot = p * SA + s
         for found_in, mine, code_of in (
             (found[0], way == 0, code(a_slot, part, (p & 1) * 8 + t, c_slot)),
-            (found[1], sent, code(a_slot, sent_part, sent_at, c_slot)),
+            (found[1], sent, code(a_slot, (way - 1) & 3, rank, c_slot)),
             (found[2], (way > 0) & ~sent, code(a_slot, 0, p * 8 + t, c_slot)),
         ):
             found_in.append(jnp.where(live & mine, code_of, -1).astype(jnp.float32))
@@ -292,16 +313,13 @@
     lax.fori_loop(0, count, step, 0)
 
 
-def own_kernel(me_ref, info_ref, a_ref, *rest):
-    b_refs, (out_ref, sent_list, own_list, *buffers) = rest[:3], rest[3:]
-    here, sent, _ = entries_of(info_ref, me_ref[0])
-    extract(here, own_list)
+def own_kernel(list_ref, a_ref, *rest):
+    b_refs, (out_ref, *buffers) = rest[:3], rest[3:]
 
     def meanwhile():
-        extract(sent, sent_list)
         out_ref[...] = jnp.zeros_like(out_ref)
 
-    multiply_listed(own_list, a_ref, b_refs, out_ref, *buffers, meanwhile)
+    multiply_listed(list_ref, a_ref, b_refs, out_ref, *buffers, meanwhile)
 
 
 def sent_kernel(list_ref, a_ref, *rest):
@@ -322,21 +340,19 @@
     multiply_listed(rest_list, a_ref, [b_ref], out_ref, *buffers, meanwhile)
 
 
-def products(kernel, leading, a_all, b_parts, total, slots, lists_out=False, lists=True):
+def products(kernel, leading, a_all, b_parts, total, slots, own_list=False):
     size = a_all.shape[-1]
     smem = pl.BlockSpec(memory_space=pltpu.SMEM)
     vmem = pl.BlockSpec(memory_space=pltpu.VMEM)
     operands = [*leading, a_all, *b_parts] + ([] if total is None else [total])
-    out = jax.ShapeDtypeStruct((slots, size, size), jnp.float32)
-    listing = (LIST + 1,)
     return pl.pallas_call(
         kernel,
         in_specs=[smem if x.ndim == 1 else vmem for x in leading]
         + [pl.BlockSpec(memory_space=pl.ANY)] * (1 + len(b_parts))
         + ([] if total is None else [vmem]),
-        out_specs=[vmem, smem] if lists_out else vmem,
-        out_shape=[out, jax.ShapeDtypeStruct(listing, jnp.int32)] if lists_out else out,
-        scratch_shapes=([pltpu.SMEM(listing, jnp.int32)] if lists else [])
+        out_specs=vmem,
+        out_shape=jax.ShapeDtypeStruct((slots, size, size), jnp.float32),
+        scratch_shapes=([pltpu.SMEM((LIST + 1,), jnp.int32)] if own_list else [])
         + [
             pltpu.VMEM((AHEAD, size, size), jnp.float32),
             pltpu.VMEM((AHEAD, size, size), jnp.float32),
@@ -394,28 +410,27 @@
     mine = jnp.concatenate([a_index[0, 0], blank, b_index[0, 0].reshape(-1), c_index[0, 0]])
     spots = everywhere(jnp.pad(mine, (0, 128 - mine.shape[0])), rows, columns)
 
-    order = jnp.asarray(lane_order(rows, columns))
-    maps = jnp.asarray(lane_maps(columns, hold, rows))
-
     sends = [
-        (NEAR, 1, 0, lambda i: i ^ 1),
-        (AHEAD_FAR, 2, 0, lambda i: (i + 2) & 7),
-        (BEHIND_FAR, 2, AHEAD_FAR, lambda i: (i - 2) & 7),
-        (AHEAD_FAR, 3, 0, lambda i: ((i + 2) & 7) ^ 1),
-        (BEHIND_FAR, 3, AHEAD_FAR, lambda i: ((i - 2) & 7) ^ 1),
+        (FAR, 2, lambda i: (i + 2) & 7),
+        (FAR, 3, lambda i: ((i + 2) & 7) ^ 1),
+        (NEAR, 1, lambda i: i ^ 1),
     ]
-    *packed, info = pack(me, spots, order, maps, near, sends)
-    arrived = [to_row(block, rows, there) for block, (*_, there) in zip(packed, sends)]
-
-    total, sent_list = products(own_kernel, [me, info], a_all, near, None, sc, lists_out=True)
-    total = products(sent_kernel, [sent_list], a_all, arrived, total, sc, lists=False)
-
-    trips = overflow(spots, order, maps)[0]
+    pack_list, own_list, sent_list, info, maps = plan(me, spots, sends)
+    packed = pack(pack_list, near, [n for n, *_ in sends])
+    far_own, far_other, cross = [
+        to_row(block, rows, there) for block, (*_, there) in zip(packed, sends)
+    ]
+
+    total = products(own_kernel, [own_list], a_all, near, None, sc)
+    total = products(sent_kernel, [sent_list], a_all, [cross, far_own, far_other], total, sc)
+
+    trips = overflow(spots, maps)[0]
 
     def trip(state):
         done, total = state
         whole = lax.all_gather(own, "row").reshape(rows * held, size, size)
-        return done + 1, products(rest_kernel, [me, info], a_all, [whole], total, sc)
+        rest = products(rest_kernel, [me, info], a_all, [whole], total, sc, own_list=True)
+        return done + 1, rest
 
     _, total = lax.while_loop(lambda state: state[0] < trips, trip, (jnp.int32(0), total))
     return total[None, None]

time: 71.9 us -> 72.6 us (level); the launches traced: 70.8 us -> 73 us
  waiting for transfers between devices: 13.6 us -> 21.8 us
  starting transfers between devices: 29.3 us -> 23.1 us
  Pallas kernels: 9.37 us -> 11.3 us
  local copies, waits for them, and re-layouts: 3.65 us -> 1.97 us
    ppermute x7 -> x5, starting transfers between devices: 11.6 us -> 5.42 us  [to_row(): return lax.ppermute(block, 'row', [(i, there(i)) for i in range(rows)])]
    ppermute x7 -> x5, waiting for transfers between devices: 4.79 us -> 9.07 us  [to_row(): return lax.ppermute(block, 'row', [(i, there(i)) for i in range(rows)])]
    all_gather x1, waiting for transfers between devices: 0.02 us -> 3.93 us  [per_device(): lax.all_gather(a_blocks[0, 0], COL).reshape(columns * sa, size, size)]
    pallas_call x2 -> x3, Pallas kernels: 4.64 us -> 6.7 us  [the longest x1 2.75 us: plan(): pl.pallas_call(functools.partial(plan_kernel, sends), in_specs=[smem, vme...]
    unnamed x8 -> x4, local copies, waits for them, and re-layouts: 2.64 us -> 0.97 us
  transfers between devices with their start and end apart: 18 -> 16, of which waited for: 8 -> 8; matrix products, arithmetic and copies ran while one was open for 3% -> 2% of each run, Pallas kernels for 11% -> 12%
where the time goes in v1:
time: 72.6 us; the launch traced here: 73 us
  starting transfers between devices  23.1 us (32%)
  waiting for transfers between devices  21.8 us (30%)
  between operations  13.5 us (19%)
  Pallas kernels  11.3 us (16%)
  local copies, waits for them, and re-layouts  1.97 us (3%)
  other arithmetic  0.82 us (1%)
    ppermute x10, starting transfers between devices, everywhere(): lax.ppermute(held, axes, [(i ^ flip, i) for i in range(rows * columns)])  17.7 us
    ppermute x5, waiting for transfers between devices, to_row(): return lax.ppermute(block, 'row', [(i, there(i)) for i in range(rows)])  9.07 us
    ppermute x10, waiting for transfers between devices, everywhere(): lax.ppermute(held, axes, [(i ^ flip, i) for i in range(rows * columns)])  8.03 us
    ppermute x5, starting transfers between devices, to_row(): return lax.ppermute(block, 'row', [(i, there(i)) for i in range(rows)])  5.42 us
    pallas_call x2, Pallas kernels, products(): pl.pallas_call(kernel, in_specs=[smem if x.ndim == 1 else vmem for x in l...  4.56 us
    all_gather x1, waiting for transfers between devices, per_device(): lax.all_gather(a_blocks[0, 0], COL).reshape(columns * sa, size, size)  3.93 us
    pallas_call x1, Pallas kernels, plan(): pl.pallas_call(functools.partial(plan_kernel, sends), in_specs=[smem, vme...  2.75 us
    pallas_call x1, Pallas kernels, pack(): pl.pallas_call(functools.partial(pack_kernel, sizes), in_specs=[pl.BlockS...  2.22 us
  transfers between devices with their start and end apart: 16, of which 8 were waited for; matrix products, arithmetic and copies ran while one was open for 2% of the time, Pallas kernels for 12%

profile of v1, /device:TPU:1, one launch (start us, length us, event | category | flops | bytes accessed | tf_op | source)
XLA Modules:
  0.0 73.0 jit_solution(6887613459040072778)
XLA Ops:
  6.5 0.0 all-gather.4.cloned.1.call-start
  6.5 0.7 all-gather.4.cloned.1.call-update
  7.3 0.8 %reshape_squeeze.6 = s32[16]{0:T(128)S(1)} reshape(s32[1,1,2,8]{3,2,1,0:T(2,128)} %param.10) | data formatting | bytes 128 | tf_op jit(solution)/shard_map/reshape;squeeze | solution.py:410
  8.0 0.7 %pad_add_fusion.1 = s32[40]{0:T(128)S(1)} fusion(s32[16]{0:T(128)} %bitcast.51, s32[16]{0:T(128)S(1)} %reshape_squeeze.6, s32[4]{0:T(128)S(1)} %broadcast.5, s32[4]{0:T(128)} %bitcast.52), kind=kLoop, calls=%fused_computation.11 | loop fusion | flops 120 | bytes 320 | tf_op jit(solution)/shard_map/concatenate | solution.py:410
  8.8 3.8 %collective-permute-start.1 = (s32[128]{0:T(128)S(1)}, s32[128]{0:T(128)S(1)}, u32[]{:S(2)}, u32[]{:S(2)}) collective-permute-start(s32[128]{0:T(128)S(1)} %get-tuple-element.74), channel_id=1, source_target_pairs={{64,0},{65,1},{66,2},{67,3},{68,4},{69,5},{70,6},{71,7},{72,8},{73... | collective-permute-start | bytes 1544 | tf_op jit(solution)/shard_map/ppermute | solution.py:385
  12.5 0.4 collective-permute-start
  12.9 0.4 collective-permute-start.2
  13.3 2.3 %collective-permute-start.11 = (f32[16,128,128]{2,1,0:T(8,128)}, f32[16,128,128]{2,1,0:T(8,128)S(1)}, u32[]{:S(2)}, u32[]{:S(2)}) collective-permute-start(f32[16,128,128]{2,1,0:T(8,128)} %bitcast.46), channel_id=1, source_target_pairs={{0,96},{16,112},{32,0},{48,16},{64,32},{80,48},{96,64},{112,80},{1... | collective-permute-start | bytes 3145736 | tf_op jit(solution)/shard_map/ppermute | solution.py:372
  15.6 0.0 collective-permute-start.10
  15.6 0.1 pad_add_fusion.me_ref
  15.7 0.0 collective-permute-done
  15.8 0.0 collective-permute-done.1
  15.8 0.7 %collective-permute-done.2 = s32[128]{0:T(128)S(1)} collective-permute-done((s32[128]{0:T(128)S(1)}, s32[128]{0:T(128)S(1)}, u32[]{:S(2)}, u32[]{:S(2)}) %collective-permute-start.2) | collective-permute-done | bytes 544 | tf_op jit(solution)/shard_map/ppermute | solution.py:385
  16.6 2.5 %collective-permute-start.5 = (s32[4,128]{1,0:T(4,128)S(1)}, s32[4,128]{1,0:T(4,128)S(1)}, u32[]{:S(2)}, u32[]{:S(2)}) collective-permute-start(s32[4,128]{1,0:T(4,128)S(1)} %dynamic_update_slice.49), channel_id=1, source_target_pairs={{24,0},{25,1},{26,2},{27,3},{28,4},{29,5},{30,6},{31,7},{16,8},{17... | collective-permute-start | bytes 6152 | tf_op jit(solution)/shard_map/ppermute | solution.py:385
  19.1 0.5 collective-permute-start.4
  19.6 0.3 collective-permute-start.3
  19.9 2.5 %collective-permute-done.3 = s32[4,128]{1,0:T(4,128)S(1)} collective-permute-done((s32[4,128]{1,0:T(4,128)S(1)}, s32[4,128]{1,0:T(4,128)S(1)}, u32[]{:S(2)}, u32[]{:S(2)}) %collective-permute-start.3) | collective-permute-done | bytes 2080 | tf_op jit(solution)/shard_map/ppermute | solution.py:385
  22.4 0.7 collective-permute-done.4
  23.1 0.0 collective-permute-done.5
  23.1 3.8 %collective-permute-start.8 = (s32[4,4,128]{2,1,0:T(4,128)S(1)}, s32[4,4,128]{2,1,0:T(4,128)S(1)}, u32[]{:S(2)}, u32[]{:S(2)}) collective-permute-start(s32[4,4,128]{2,1,0:T(4,128)S(1)} %constant_dynamic-update-slice_fusion), channel_id=1, source_target_pairs={{6,0},{7,1},{4,2},{5,3},{2,4},{3,5},{0,6},{1,7},{14,8},{15,9},{12,... | collective-permute-start | bytes 24584 | tf_op jit(solution)/shard_map/ppermute | solution.py:385
  26.9 0.0 collective-permute-start.7
  26.9 0.7 collective-permute-start.6
  27.6 2.2 %collective-permute-done.6 = s32[4,4,128]{2,1,0:T(4,128)S(1)} collective-permute-done((s32[4,4,128]{2,1,0:T(4,128)S(1)}, s32[4,4,128]{2,1,0:T(4,128)S(1)}, u32[]{:S(2)}, u32[]{:S(2)}) %collective-permute-start.6) | collective-permute-done | bytes 8224 | tf_op jit(solution)/shard_map/ppermute | solution.py:385
  29.8 1.1 %collective-permute-done.7 = s32[4,4,128]{2,1,0:T(4,128)S(1)} collective-permute-done((s32[4,4,128]{2,1,0:T(4,128)S(1)}, s32[4,4,128]{2,1,0:T(4,128)S(1)}, u32[]{:S(2)}, u32[]{:S(2)}) %collective-permute-start.7) | collective-permute-done | bytes 8224 | tf_op jit(solution)/shard_map/ppermute | solution.py:385
  30.9 0.0 collective-permute-done.8
  30.9 5.3 %collective-permute-start.9 = (s32[4,4,4,128]{3,2,1,0:T(4,128)S(1)}, s32[4,4,4,128]{3,2,1,0:T(4,128)S(1)}, u32[]{:S(2)}, u32[]{:S(2)}) collective-permute-start(s32[4,4,4,128]{3,2,1,0:T(4,128)S(1)} %bitcast_dynamic-update-slice_fusion.2), channel_id=1, source_target_pairs={{1,0},{0,1},{3,2},{2,3},{5,4},{4,5},{7,6},{6,7},{9,8},{8,9},{11,10... | collective-permute-start | bytes 98312 | tf_op jit(solution)/shard_map/ppermute | solution.py:385
  36.3 0.8 %collective-permute-done.9 = s32[4,4,4,128]{3,2,1,0:T(4,128)S(1)} collective-permute-done((s32[4,4,4,128]{3,2,1,0:T(4,128)S(1)}, s32[4,4,4,128]{3,2,1,0:T(4,128)S(1)}, u32[]{:S(2)}, u32[]{:S(2)}) %collective-permute-start.9) | collective-permute-done | bytes 32800 | tf_op jit(solution)/shard_map/ppermute | solution.py:385
  37.1 2.8 %plan.1 = (s32[12]{0:T(128)S(1)}, s32[513]{0:T(1024)S(1)}, s32[513]{0:T(1024)S(1)}, s32[40,128]{1,0:T(8,128)S(1)}, bf16[6,128,128]{2,1,0:T(8,128)(2,1)S(1)}) custom-call(s32[2]{0:T(128)S(1)} %pad_add_fusion.me_ref, s32[128,128]{1,0:T(8,128)S(1)} %bitcast.41), custom_call_target="tpu_custom_call" | custom-call | tf_op jit(solution)/shard_map/plan/pallas_call | solution.py:153
  39.9 0.0 collective-permute-done.11.rest_2_
  39.9 0.0 collective-permute-done.10.rest_1_
  39.9 2.2 %pack.1 = (f32[3,128,128]{2,1,0:T(8,128)}, f32[3,128,128]{2,1,0:T(8,128)S(1)}, f32[6,128,128]{2,1,0:T(8,128)S(1)}) custom-call(s32[12]{0:T(128)S(1)} %get-tuple-element.52.list_ref, f32[16,128,128]{2,1,0:T(8,128)} %bitcast.48, f32[16,128,128]{2,1,0:T(8,128)S(1)} %collective-permute-done.10.rest_1_, f32[16,128,128]{2,1,0:T(8,128)S(1)} %collective-permute-done.11.rest_2_), custom_call_target="tpu_custom_call" | custom-call | tf_op jit(solution)/shard_map/pack/pallas_call | solution.py:188
  42.2 3.1 %collective-permute-start.12 = (f32[6,128,128]{2,1,0:T(8,128)S(1)}, f32[6,128,128]{2,1,0:T(8,128)S(1)}, u32[]{:S(2)}, u32[]{:S(2)}) collective-permute-start(f32[6,128,128]{2,1,0:T(8,128)S(1)} %get-tuple-element.53), channel_id=1, source_target_pairs={{0,16},{16,0},{32,48},{48,32},{64,80},{80,64},{96,112},{112,96},{1... | collective-permute-start | bytes 1179656 | tf_op jit(solution)/shard_map/ppermute | solution.py:372
  45.3 0.0 collective-permute-start.13
  45.3 0.0 collective-permute-start.14
  45.3 1.7 %overflow.1 = s32[1]{0:T(128)} custom-call(s32[128,128]{1,0:T(8,128)S(1)} %bitcast.42, bf16[6,128,128]{2,1,0:T(8,128)(2,1)S(1)} %get-tuple-element.57.maps_ref), custom_call_target="tpu_custom_call" | custom-call | flops 1000000000 | bytes 100000 | tf_op jit(solution)/shard_map/overflow/pallas_call | solution.py:223
  47.0 3.9 %all-gather.4.cloned.1.call-done = f32[16,1,4,128,128]{4,3,2,1,0:T(8,128)} async-done(((f32[1,1,4,128,128]{4,3,2,1,0:T(8,128)}), f32[16,1,4,128,128]{4,3,2,1,0:T(8,128)}) %all-gather.4.cloned.1.call-update) | async-done | bytes 4194320 | tf_op jit(solution)/shard_map/all_gather | solution.py:402
  50.9 0.0 copy-start.1
  50.9 2.2 %products.3.rest_3_ = f32[16,128,128]{2,1,0:T(8,128)S(1)} custom-call(s32[513]{0:T(1024)S(1)} %get-tuple-element.56.list_ref, f32[64,128,128]{2,1,0:T(8,128)} %bitcast.43, f32[16,128,128]{2,1,0:T(8,128)} %bitcast.49, f32[16,128,128]{2,1,0:T(8,128)S(1)} %collective-permute-done.10.rest_1_, f32[16,128,128]{2,1,0:T(8,128)S(1)} %collective-permute-done.11.rest_2_), custom_call_target="tpu_custom_call" | custom-call | flops 100663296 | bytes 1572864 | tf_op jit(solution)/shard_map/products/pallas_call | solution.py:348
  53.2 0.0 collective-permute-done.13.rest_1_
  53.2 9.1 %collective-permute-done.14.rest_2_ = f32[3,128,128]{2,1,0:T(8,128)S(1)} collective-permute-done((f32[3,128,128]{2,1,0:T(8,128)S(1)}, f32[3,128,128]{2,1,0:T(8,128)S(1)}, u32[]{:S(2)}, u32[]{:S(2)}) %collective-permute-start.14) | collective-permute-done | bytes 196640 | tf_op jit(solution)/shard_map/ppermute | solution.py:372
  62.2 0.0 collective-permute-done.12.rest_0_
  62.2 0.0 copy-done.1
  62.2 2.4 %products.4 = f32[16,128,128]{2,1,0:T(8,128)S(1)} custom-call(s32[513]{0:T(1024)S(1)} %get-tuple-element.51.list_ref, f32[64,128,128]{2,1,0:T(8,128)S(1)} %bitcast.45, f32[6,128,128]{2,1,0:T(8,128)S(1)} %collective-permute-done.12.rest_0_, f32[3,128,128]{2,1,0:T(8,128)S(1)} %collective-permute-done.13.rest_1_, ...), custom_call_target="tpu_custom_call", output_to_operand_aliasing={{}: (5, {})} | custom-call | flops 100663296 | bytes 1572864 | tf_op jit(solution)/shard_map/products/pallas_call | solution.py:348
  64.6 0.0 copy-start.2
  64.6 1.0 %copy-done.2 = f32[16,128,128]{2,1,0:T(8,128)} copy-done((f32[16,128,128]{2,1,0:T(8,128)}, f32[16,128,128]{2,1,0:T(8,128)S(1)}, u32[]{:S(2)}) %copy-start.2) | copy-done | bytes 1048600
  65.6 0.6 while.10
  (20 shorter events, 0.2 us)
Async XLA Ops:
  6.5 44.4 %all-gather.4.cloned.1.call-start = ((), (), s32[]{:S(2)}) async-start(), calls=%async_computation | async-start | bytes 4456448 | tf_op jit(solution)/shard_map/all_gather | solution.py:402
  8.8 7.0 %collective-permute-start.1 = (s32[128]{0:T(128)S(1)}, s32[128]{0:T(128)S(1)}, u32[]{:S(2)}, u32[]{:S(2)}) collective-permute-start(s32[128]{0:T(128)S(1)} %get-tuple-element.74), channel_id=1, source_target_pairs={{64,0},{65,1},{66,2},{67,3},{68,4},{69,5},{70,6},{71,7},{72,8},{73... | collective-permute-start | bytes 1544 | tf_op jit(solution)/shard_map/ppermute | solution.py:385
  12.5 3.2 %collective-permute-start = (s32[128]{0:T(128)S(1)}, s32[128]{0:T(128)S(1)}, u32[]{:S(2)}, u32[]{:S(2)}) collective-permute-start(s32[128]{0:T(128)S(1)} %get-tuple-element.74), channel_id=1, source_target_pairs={{32,0},{33,1},{34,2},{35,3},{36,4},{37,5},{38,6},{39,7},{40,8},{41... | collective-permute-start | bytes 1544 | tf_op jit(solution)/shard_map/ppermute | solution.py:385
  12.9 3.6 %collective-permute-start.2 = (s32[128]{0:T(128)S(1)}, s32[128]{0:T(128)S(1)}, u32[]{:S(2)}, u32[]{:S(2)}) collective-permute-start(s32[128]{0:T(128)S(1)} %get-tuple-element.74), channel_id=1, source_target_pairs={{96,0},{97,1},{98,2},{99,3},{100,4},{101,5},{102,6},{103,7},{104,8... | collective-permute-start | bytes 1544 | tf_op jit(solution)/shard_map/ppermute | solution.py:385
  13.3 26.6 %collective-permute-start.11 = (f32[16,128,128]{2,1,0:T(8,128)}, f32[16,128,128]{2,1,0:T(8,128)S(1)}, u32[]{:S(2)}, u32[]{:S(2)}) collective-permute-start(f32[16,128,128]{2,1,0:T(8,128)} %bitcast.46), channel_id=1, source_target_pairs={{0,96},{16,112},{32,0},{48,16},{64,32},{80,48},{96,64},{112,80},{1... | collective-permute-start | bytes 3145736 | tf_op jit(solution)/shard_map/ppermute | solution.py:372
  15.6 24.3 %collective-permute-start.10 = (f32[16,128,128]{2,1,0:T(8,128)}, f32[16,128,128]{2,1,0:T(8,128)S(1)}, u32[]{:S(2)}, u32[]{:S(2)}) collective-permute-start(f32[16,128,128]{2,1,0:T(8,128)} %bitcast.47), channel_id=1, source_target_pairs={{0,32},{16,48},{32,64},{48,80},{64,96},{80,112},{96,0},{112,16},{1... | collective-permute-start | bytes 3145736 | tf_op jit(solution)/shard_map/ppermute | solution.py:372
  16.6 6.5 %collective-permute-start.5 = (s32[4,128]{1,0:T(4,128)S(1)}, s32[4,128]{1,0:T(4,128)S(1)}, u32[]{:S(2)}, u32[]{:S(2)}) collective-permute-start(s32[4,128]{1,0:T(4,128)S(1)} %dynamic_update_slice.49), channel_id=1, source_target_pairs={{24,0},{25,1},{26,2},{27,3},{28,4},{29,5},{30,6},{31,7},{16,8},{17... | collective-permute-start | bytes 6152 | tf_op jit(solution)/shard_map/ppermute | solution.py:385
  19.1 3.9 %collective-permute-start.4 = (s32[4,128]{1,0:T(4,128)S(1)}, s32[4,128]{1,0:T(4,128)S(1)}, u32[]{:S(2)}, u32[]{:S(2)}) collective-permute-start(s32[4,128]{1,0:T(4,128)S(1)} %dynamic_update_slice.49), channel_id=1, source_target_pairs={{16,0},{17,1},{18,2},{19,3},{20,4},{21,5},{22,6},{23,7},{24,8},{25... | collective-permute-start | bytes 6152 | tf_op jit(solution)/shard_map/ppermute | solution.py:385
  19.6 2.7 %collective-permute-start.3 = (s32[4,128]{1,0:T(4,128)S(1)}, s32[4,128]{1,0:T(4,128)S(1)}, u32[]{:S(2)}, u32[]{:S(2)}) collective-permute-start(s32[4,128]{1,0:T(4,128)S(1)} %dynamic_update_slice.49), channel_id=1, source_target_pairs={{8,0},{9,1},{10,2},{11,3},{12,4},{13,5},{14,6},{15,7},{0,8},{1,9},... | collective-permute-start | bytes 6152 | tf_op jit(solution)/shard_map/ppermute | solution.py:385
  23.1 7.9 %collective-permute-start.8 = (s32[4,4,128]{2,1,0:T(4,128)S(1)}, s32[4,4,128]{2,1,0:T(4,128)S(1)}, u32[]{:S(2)}, u32[]{:S(2)}) collective-permute-start(s32[4,4,128]{2,1,0:T(4,128)S(1)} %constant_dynamic-update-slice_fusion), channel_id=1, source_target_pairs={{6,0},{7,1},{4,2},{5,3},{2,4},{3,5},{0,6},{1,7},{14,8},{15,9},{12,... | collective-permute-start | bytes 24584 | tf_op jit(solution)/shard_map/ppermute | solution.py:385
  26.9 4.0 %collective-permute-start.7 = (s32[4,4,128]{2,1,0:T(4,128)S(1)}, s32[4,4,128]{2,1,0:T(4,128)S(1)}, u32[]{:S(2)}, u32[]{:S(2)}) collective-permute-start(s32[4,4,128]{2,1,0:T(4,128)S(1)} %constant_dynamic-update-slice_fusion), channel_id=1, source_target_pairs={{4,0},{5,1},{6,2},{7,3},{0,4},{1,5},{2,6},{3,7},{12,8},{13,9},{14,... | collective-permute-start | bytes 24584 | tf_op jit(solution)/shard_map/ppermute | solution.py:385
  26.9 2.9 %collective-permute-start.6 = (s32[4,4,128]{2,1,0:T(4,128)S(1)}, s32[4,4,128]{2,1,0:T(4,128)S(1)}, u32[]{:S(2)}, u32[]{:S(2)}) collective-permute-start(s32[4,4,128]{2,1,0:T(4,128)S(1)} %constant_dynamic-update-slice_fusion), channel_id=1, source_target_pairs={{2,0},{3,1},{0,2},{1,3},{6,4},{7,5},{4,6},{5,7},{10,8},{11,9},{8,1... | collective-permute-start | bytes 24584 | tf_op jit(solution)/shard_map/ppermute | solution.py:385
  30.9 6.2 %collective-permute-start.9 = (s32[4,4,4,128]{3,2,1,0:T(4,128)S(1)}, s32[4,4,4,128]{3,2,1,0:T(4,128)S(1)}, u32[]{:S(2)}, u32[]{:S(2)}) collective-permute-start(s32[4,4,4,128]{3,2,1,0:T(4,128)S(1)} %bitcast_dynamic-update-slice_fusion.2), channel_id=1, source_target_pairs={{1,0},{0,1},{3,2},{2,3},{5,4},{4,5},{7,6},{6,7},{9,8},{8,9},{11,10... | collective-permute-start | bytes 98312 | tf_op jit(solution)/shard_map/ppermute | solution.py:385
  42.2 20.1 %collective-permute-start.12 = (f32[6,128,128]{2,1,0:T(8,128)S(1)}, f32[6,128,128]{2,1,0:T(8,128)S(1)}, u32[]{:S(2)}, u32[]{:S(2)}) collective-permute-start(f32[6,128,128]{2,1,0:T(8,128)S(1)} %get-tuple-element.53), channel_id=1, source_target_pairs={{0,16},{16,0},{32,48},{48,32},{64,80},{80,64},{96,112},{112,96},{1... | collective-permute-start | bytes 1179656 | tf_op jit(solution)/shard_map/ppermute | solution.py:372
  45.3 7.9 %collective-permute-start.13 = (f32[3,128,128]{2,1,0:T(8,128)}, f32[3,128,128]{2,1,0:T(8,128)S(1)}, u32[]{:S(2)}, u32[]{:S(2)}) collective-permute-start(f32[3,128,128]{2,1,0:T(8,128)} %get-tuple-element.54), channel_id=1, source_target_pairs={{0,32},{16,48},{32,64},{48,80},{64,96},{80,112},{96,0},{112,16},{1... | collective-permute-start | bytes 589832 | tf_op jit(solution)/shard_map/ppermute | solution.py:372
  45.3 17.0 %collective-permute-start.14 = (f32[3,128,128]{2,1,0:T(8,128)S(1)}, f32[3,128,128]{2,1,0:T(8,128)S(1)}, u32[]{:S(2)}, u32[]{:S(2)}) collective-permute-start(f32[3,128,128]{2,1,0:T(8,128)S(1)} %get-tuple-element.55), channel_id=1, source_target_pairs={{0,48},{16,32},{32,80},{48,64},{64,112},{80,96},{96,16},{112,0},{1... | collective-permute-start | bytes 589832 | tf_op jit(solution)/shard_map/ppermute | solution.py:372
  50.9 11.3 %copy-start.1 = (f32[16,1,4,128,128]{4,3,2,1,0:T(8,128)S(1)}, f32[16,1,4,128,128]{4,3,2,1,0:T(8,128)}, u32[]{:S(2)}) copy-start(f32[16,1,4,128,128]{4,3,2,1,0:T(8,128)} %all-gather.4.cloned.1.call-done) | copy-start | bytes 12582916
  64.6 1.0 %copy-start.2 = (f32[16,128,128]{2,1,0:T(8,128)}, f32[16,128,128]{2,1,0:T(8,128)S(1)}, u32[]{:S(2)}) copy-start(f32[16,128,128]{2,1,0:T(8,128)S(1)} %products.4) | copy-start | bytes 3145732
Sparse Core Ops, SparseCore 0:
  9.1 41.8 all-gather.3

commit v2 on v1

--- a/solution.py
+++ b/solution.py
@@ -11,8 +11,7 @@
 SA = 4
 PK = 8
 NBD = 8
-NEAR = 6
-FAR = 3
+SLOTS = 5
 COL = ("x_lo", "z", "core")
 LIST = 512
 AHEAD = 8
@@ -40,8 +39,7 @@
     lane = lax.broadcasted_iota(jnp.int32, shape, axis)
     r, p = lane >> 4, lane & 15
     owner = p >> 1
-    far = (((owner >> 1) - (r >> 1)) & 3) == 2
-    way = ((owner ^ r) & 1) + jnp.where(far, 2, 0)
+    way = ((owner >> 1) - (r >> 1)) & 3
     return r, p, owner, way
 
 
@@ -86,7 +84,7 @@
     holder = (p_down == 0) & (r_down == owner)
     alike = (r == r_down) & (way == way_down)
     y, xh, xl, z, core = lane >> 5, (lane >> 4) & 1, (lane >> 3) & 1, (lane >> 1) & 3, lane & 1
-    listed_at = (((core * 4 + z) * 2 + xh) * 2 + xl) * 4 + y
+    listed_at = (((core * 4 + z) * 4 + y) * 2 + xh) * 2 + xl
     for n, flags in enumerate(
         [
             holder & ((p & 1) == 0),
@@ -128,12 +126,10 @@
     rank = (upto - alike + matmul(flags, maps_ref[4])).astype(jnp.int32)
     order = jnp.where(need, way * 128 + rank, -1)
 
-    steps = ((owner >> 1) - (row >> 1)) & 3
-    part = jnp.where(steps == 0, 0, jnp.where(steps == 3, 1, 2))
-    word = (part * 16 + (p & 1) * 8 + t).astype(jnp.float32)
+    word = (((owner ^ row) & 1) * 16 + (p & 1) * 8 + t).astype(jnp.float32)
     n = 0
-    for slots, which, there in sends:
-        for e in range(slots):
+    for which, there in sends:
+        for e in range(SLOTS):
             hit = (order == which * 128 + e) & (r == there(row))
             pack_list[n] = jnp.max(jnp.where(hit, word, -1.0)).astype(jnp.int32)
             n += 1
@@ -155,7 +151,7 @@
         in_specs=[smem, vmem],
         out_specs=[smem, smem, smem, vmem, vmem],
         out_shape=[
-            jax.ShapeDtypeStruct((sum(n for n, *_ in sends),), jnp.int32),
+            jax.ShapeDtypeStruct((len(sends) * SLOTS,), jnp.int32),
             jax.ShapeDtypeStruct((LIST + 1,), jnp.int32),
             jax.ShapeDtypeStruct((LIST + 1,), jnp.int32),
             jax.ShapeDtypeStruct((40, 128), jnp.int32),
@@ -166,9 +162,9 @@
     )(me, spots)
 
 
-def pack_kernel(sizes, list_ref, *rest):
-    near, packed, sems = rest[:3], rest[3:-1], rest[-1]
-    places = [(i, e) for i, size in enumerate(sizes) for e in range(size)]
+def pack_kernel(parts, list_ref, *rest):
+    near, packed, sems = rest[:parts], rest[parts:-1], rest[-1]
+    places = [(i, e) for i in range(len(packed)) for e in range(SLOTS)]
     for n, (i, e) in enumerate(places):
         word = list_ref[n]
 
@@ -183,15 +179,15 @@
             pltpu.make_async_copy(near[0].at[0], packed[i].at[e], sems.at[n]).wait()
 
 
-def pack(listing, near, sizes):
+def pack(listing, near, sends):
     size = near[0].shape[-1]
     return pl.pallas_call(
-        functools.partial(pack_kernel, sizes),
+        functools.partial(pack_kernel, len(near)),
         in_specs=[pl.BlockSpec(memory_space=pltpu.SMEM)]
-        + [pl.BlockSpec(memory_space=pl.ANY)] * 3,
-        out_specs=[pl.BlockSpec(memory_space=pltpu.VMEM)] * len(sizes),
-        scratch_shapes=[pltpu.SemaphoreType.DMA((sum(sizes),))],
-        out_shape=[jax.ShapeDtypeStruct((n, size, size), jnp.float32) for n in sizes],
+        + [pl.BlockSpec(memory_space=pl.ANY)] * len(near),
+        out_specs=[pl.BlockSpec(memory_space=pltpu.VMEM)] * len(sends),
+        scratch_shapes=[pltpu.SemaphoreType.DMA((len(sends) * SLOTS,))],
+        out_shape=[jax.ShapeDtypeStruct((SLOTS, size, size), jnp.float32)] * len(sends),
         compiler_params=pltpu.CompilerParams(vmem_limit_bytes=16 << 20),
         name="pack",
     )(listing, *near)
@@ -214,7 +210,7 @@
     for q in range(1, 16):
         most = jnp.maximum(most, jnp.sum(alike[q * 8 : q * 8 + 8], axis=0, keepdims=True))
     *_, way = lane_facts(most.shape)
-    slots = jnp.where(way == 0, 128, jnp.where(way == 1, NEAR, FAR))
+    slots = jnp.where(way == 0, 128, SLOTS)
     over_ref[0] = jnp.max(jnp.where(most > slots.astype(jnp.float32), 1.0, 0.0)).astype(jnp.int32)
 
 
@@ -261,9 +257,8 @@
     r, p, owner, way = lane_facts(b.shape)
     t = lax.broadcasted_iota(jnp.int32, b.shape, 0)
     rank = order & 127
-    steps = ((owner >> 1) - (row >> 1)) & 3
-    part = jnp.where(steps == 0, 0, jnp.where(steps == 3, 1, 2))
-    sent = (way > 0) & (rank < jnp.where(way == 1, NEAR, FAR))
+    part = (owner ^ row) & 1
+    sent = (way > 0) & (rank < SLOTS)
     found = [[], [], []]
     for s in range(SA):
         lands = lands_at(info_ref[s : s + 1], b)
@@ -281,7 +276,7 @@
     return [jnp.concatenate(x) for x in found]
 
 
-def multiply_listed(list_ref, a_ref, b_refs, out_ref, a_buf, b_buf, a_sem, b_sem, meanwhile):
+def multiply_listed(list_ref, a_ref, b_refs, acc, a_buf, b_buf, a_sem, b_sem, meanwhile):
     count = list_ref[LIST]
 
     def fetch(n):
@@ -302,7 +297,7 @@
         slot = n % AHEAD
         pltpu.make_async_copy(a_ref.at[0], a_buf.at[slot], a_sem.at[slot]).wait()
         pltpu.make_async_copy(b_refs[0].at[0], b_buf.at[slot], b_sem.at[slot]).wait()
-        out_ref[c_of(list_ref[n])] += block_product(a_buf[slot], b_buf[slot])
+        acc[c_of(list_ref[n])] += block_product(a_buf[slot], b_buf[slot])
 
         @pl.when(n + AHEAD < count)
         def _():
@@ -313,47 +308,80 @@
     lax.fori_loop(0, count, step, 0)
 
 
-def own_kernel(list_ref, a_ref, *rest):
-    b_refs, (out_ref, *buffers) = rest[:3], rest[3:]
+def own_kernel(parts, list_ref, a_ref, *rest):
+    b_refs, (out_ref, acc, c_sem, _, *buffers) = rest[:parts], rest[parts:]
 
     def meanwhile():
-        out_ref[...] = jnp.zeros_like(out_ref)
-
-    multiply_listed(list_ref, a_ref, b_refs, out_ref, *buffers, meanwhile)
-
-
-def sent_kernel(list_ref, a_ref, *rest):
-    b_refs, (total_ref, out_ref, *buffers) = rest[:-6], rest[-6:]
+        acc[...] = jnp.zeros_like(acc)
+
+    multiply_listed(list_ref, a_ref, b_refs, acc, *buffers, meanwhile)
+    copy = pltpu.make_async_copy(acc, out_ref, c_sem.at[0])
+    copy.start()
+    copy.wait()
+
+
+def add_listed(list_ref, a_ref, b_refs, total_ref, out_ref, acc, c_sem, stage, *buffers):
+    count = list_ref[LIST]
+
+    def touched(was, act):
+        def step(n, carry):
+            c = c_of(list_ref[n])
+
+            @pl.when(stage[c] == was)
+            def _():
+                stage[c] = was + 1
+                act(c)
+
+            return carry
+
+        lax.fori_loop(0, count, step, 0)
+
+    def fetched(c):
+        return pltpu.make_async_copy(total_ref.at[c], acc.at[c], c_sem.at[c])
+
+    def stored(c):
+        return pltpu.make_async_copy(acc.at[c], out_ref.at[c], c_sem.at[c])
+
+    for c in range(acc.shape[0]):
+        stage[c] = 0
 
     def meanwhile():
-        out_ref[...] = total_ref[...]
-
-    multiply_listed(list_ref, a_ref, b_refs, out_ref, *buffers, meanwhile)
-
-
-def rest_kernel(me_ref, info_ref, a_ref, b_ref, total_ref, out_ref, rest_list, *buffers):
+        touched(0, lambda c: fetched(c).start())
+        touched(1, lambda c: fetched(c).wait())
+
+    multiply_listed(list_ref, a_ref, b_refs, acc, *buffers, meanwhile)
+    touched(2, lambda c: stored(c).start())
+    touched(3, lambda c: stored(c).wait())
+
+
+def sent_kernel(parts, list_ref, a_ref, *rest):
+    add_listed(list_ref, a_ref, rest[:parts], *rest[parts:])
+
+
+def rest_kernel(parts, me_ref, info_ref, a_ref, *rest):
+    b_refs, (total_ref, out_ref, rest_list, *buffers) = rest[:parts], rest[parts:]
     extract(entries_of(info_ref, me_ref[0])[2], rest_list)
-
-    def meanwhile():
-        out_ref[...] = total_ref[...]
-
-    multiply_listed(rest_list, a_ref, [b_ref], out_ref, *buffers, meanwhile)
+    add_listed(rest_list, a_ref, b_refs, total_ref, out_ref, *buffers)
 
 
 def products(kernel, leading, a_all, b_parts, total, slots, own_list=False):
     size = a_all.shape[-1]
     smem = pl.BlockSpec(memory_space=pltpu.SMEM)
     vmem = pl.BlockSpec(memory_space=pltpu.VMEM)
+    hbm = pl.BlockSpec(memory_space=pltpu.HBM)
     operands = [*leading, a_all, *b_parts] + ([] if total is None else [total])
     return pl.pallas_call(
-        kernel,
+        functools.partial(kernel, len(b_parts)),
         in_specs=[smem if x.ndim == 1 else vmem for x in leading]
         + [pl.BlockSpec(memory_space=pl.ANY)] * (1 + len(b_parts))
-        + ([] if total is None else [vmem]),
-        out_specs=vmem,
+        + ([] if total is None else [hbm]),
+        out_specs=hbm,
         out_shape=jax.ShapeDtypeStruct((slots, size, size), jnp.float32),
         scratch_shapes=([pltpu.SMEM((LIST + 1,), jnp.int32)] if own_list else [])
         + [
+            pltpu.VMEM((slots, size, size), jnp.float32),
+            pltpu.SemaphoreType.DMA((slots,)),
+            pltpu.SMEM((slots,), jnp.int32),
             pltpu.VMEM((AHEAD, size, size), jnp.float32),
             pltpu.VMEM((AHEAD, size, size), jnp.float32),
             pltpu.SemaphoreType.DMA((AHEAD,)),
@@ -376,7 +404,7 @@
     axes = ("row", *COL)
     me = lax.axis_index("row") * columns + lax.axis_index(COL)
     held = mine
-    for bits in ((5, 6), (3, 4), (1, 2), (0,)):
+    for bits in ((3, 4), (5, 6), (1, 2), (0,)):
         group = jnp.zeros((2 ** len(bits),) + held.shape, held.dtype)
         for move in range(2 ** len(bits)):
             flip = sum(((move >> n) & 1) << bit for n, bit in enumerate(bits))
@@ -402,27 +430,23 @@
     a_all = lax.all_gather(a_blocks[0, 0], COL).reshape(columns * sa, size, size)
 
     own = b_blocks[0, 0].reshape(held, size, size)
-    behind = to_row(own, rows, lambda i: (i + 2) % rows)
-    ahead = to_row(own, rows, lambda i: (i - 2) % rows)
-    near = [own, behind, ahead]
+    near = [own, to_row(own, rows, lambda i: i ^ 1)]
 
     blank = jnp.full((8 - sa,), -1, jnp.int32)
     mine = jnp.concatenate([a_index[0, 0], blank, b_index[0, 0].reshape(-1), c_index[0, 0]])
     spots = everywhere(jnp.pad(mine, (0, 128 - mine.shape[0])), rows, columns)
 
     sends = [
-        (FAR, 2, lambda i: (i + 2) & 7),
-        (FAR, 3, lambda i: ((i + 2) & 7) ^ 1),
-        (NEAR, 1, lambda i: i ^ 1),
+        (1, lambda i: (i - 2) & 7),
+        (2, lambda i: (i + 4) & 7),
+        (3, lambda i: (i + 2) & 7),
     ]
     pack_list, own_list, sent_list, info, maps = plan(me, spots, sends)
-    packed = pack(pack_list, near, [n for n, *_ in sends])
-    far_own, far_other, cross = [
-        to_row(block, rows, there) for block, (*_, there) in zip(packed, sends)
-    ]
+    packed = pack(pack_list, near, sends)
+    arrived = [to_row(block, rows, there) for block, (_, there) in zip(packed, sends)]
 
     total = products(own_kernel, [own_list], a_all, near, None, sc)
-    total = products(sent_kernel, [sent_list], a_all, [cross, far_own, far_other], total, sc)
+    total = products(sent_kernel, [sent_list], a_all, arrived, total, sc)
 
     trips = overflow(spots, maps)[0]
 

time: 72.6 us -> 86.1 us (1.19)
  the two profiles are of different devices: /device:TPU:1 before, /device:TPU:4 now
where the time goes in v2:
time: 86.1 us; the launch traced here: 87.2 us
  waiting for transfers between devices  39 us (45%)
  starting transfers between devices  19.5 us (23%)
  between operations  13.5 us (16%)
  Pallas kernels  11.8 us (14%)
  local copies, waits for them, and re-layouts  1.97 us (2%)
    ppermute x4, waiting for transfers between devices, to_row(): return lax.ppermute(block, 'row', [(i, there(i)) for i in range(rows)])  27.6 us
    ppermute x10, starting transfers between devices, everywhere(): lax.ppermute(held, axes, [(i ^ flip, i) for i in range(rows * columns)])  13.4 us
    ppermute x10, waiting for transfers between devices, everywhere(): lax.ppermute(held, axes, [(i ^ flip, i) for i in range(rows * columns)])  10.6 us
    pallas_call x2, Pallas kernels, products(): pl.pallas_call(functools.partial(kernel, len(b_parts)), in_specs=[smem if...  6.29 us
    ppermute x4, starting transfers between devices, to_row(): return lax.ppermute(block, 'row', [(i, there(i)) for i in range(rows)])  6.06 us
    pallas_call x1, Pallas kernels, plan(): pl.pallas_call(functools.partial(plan_kernel, sends), in_specs=[smem, vme...  2.88 us
    pallas_call x1, Pallas kernels, overflow(): pl.pallas_call(overflow_kernel, in_specs=[vmem] * 2, out_specs=pl.BlockSp...  1.73 us
  transfers between devices with their start and end apart: 15, of which 11 were waited for; matrix products, arithmetic and copies ran while one was open for 2% of the time, Pallas kernels for 9%

profile of v2, /device:TPU:4, one launch (start us, length us, event | category | flops | bytes accessed | tf_op | source)
XLA Modules:
  0.0 87.2 jit_solution(18085323342314477891)
XLA Ops:
  6.5 0.0 all-gather.4.cloned.1.call-start
  6.5 0.7 all-gather.4.cloned.1.call-update
  7.3 0.8 reshape_squeeze.6
  8.0 0.7 pad_add_fusion.1
  8.8 0.5 collective-permute-start.1
  9.2 2.2 %collective-permute-start = (s32[128]{0:T(128)S(1)}, s32[128]{0:T(128)S(1)}, u32[]{:S(2)}, u32[]{:S(2)}) collective-permute-start(s32[128]{0:T(128)S(1)} %get-tuple-element.74), channel_id=1, source_target_pairs={{8,0},{9,1},{10,2},{11,3},{12,4},{13,5},{14,6},{15,7},{0,8},{1,9},... | collective-permute-start | bytes 1544 | tf_op jit(solution)/shard_map/ppermute | solution.py:413
  11.4 1.5 %collective-permute-start.2 = (s32[128]{0:T(128)S(1)}, s32[128]{0:T(128)S(1)}, u32[]{:S(2)}, u32[]{:S(2)}) collective-permute-start(s32[128]{0:T(128)S(1)} %get-tuple-element.74), channel_id=1, source_target_pairs={{24,0},{25,1},{26,2},{27,3},{28,4},{29,5},{30,6},{31,7},{16,8},{17... | collective-permute-start | bytes 1544 | tf_op jit(solution)/shard_map/ppermute | solution.py:413
  12.9 0.6 collective-permute-start.10
  13.5 0.1 pad_add_fusion.me_ref
  13.6 0.0 collective-permute-done
  13.7 0.2 collective-permute-done.1
  13.9 1.1 %collective-permute-done.2 = s32[128]{0:T(128)S(1)} collective-permute-done((s32[128]{0:T(128)S(1)}, s32[128]{0:T(128)S(1)}, u32[]{:S(2)}, u32[]{:S(2)}) %collective-permute-start.2) | collective-permute-done | bytes 544 | tf_op jit(solution)/shard_map/ppermute | solution.py:413
  15.0 3.1 %collective-permute-start.5 = (s32[4,128]{1,0:T(4,128)S(1)}, s32[4,128]{1,0:T(4,128)S(1)}, u32[]{:S(2)}, u32[]{:S(2)}) collective-permute-start(s32[4,128]{1,0:T(4,128)S(1)} %dynamic_update_slice.49), channel_id=1, source_target_pairs={{96,0},{97,1},{98,2},{99,3},{100,4},{101,5},{102,6},{103,7},{104,8... | collective-permute-start | bytes 6152 | tf_op jit(solution)/shard_map/ppermute | solution.py:413
  18.1 0.6 collective-permute-start.4
  18.7 0.5 collective-permute-start.3
  19.2 3.1 %collective-permute-done.3 = s32[4,128]{1,0:T(4,128)S(1)} collective-permute-done((s32[4,128]{1,0:T(4,128)S(1)}, s32[4,128]{1,0:T(4,128)S(1)}, u32[]{:S(2)}, u32[]{:S(2)}) %collective-permute-start.3) | collective-permute-done | bytes 2080 | tf_op jit(solution)/shard_map/ppermute | solution.py:413
  22.3 0.9 collective-permute-done.4
  23.2 0.0 collective-permute-done.5
  23.2 4.1 %collective-permute-start.8 = (s32[4,4,128]{2,1,0:T(4,128)S(1)}, s32[4,4,128]{2,1,0:T(4,128)S(1)}, u32[]{:S(2)}, u32[]{:S(2)}) collective-permute-start(s32[4,4,128]{2,1,0:T(4,128)S(1)} %constant_dynamic-update-slice_fusion), channel_id=1, source_target_pairs={{6,0},{7,1},{4,2},{5,3},{2,4},{3,5},{0,6},{1,7},{14,8},{15,9},{12,... | collective-permute-start | bytes 24584 | tf_op jit(solution)/shard_map/ppermute | solution.py:413
  27.3 0.0 collective-permute-start.7
  27.3 0.9 %collective-permute-start.6 = (s32[4,4,128]{2,1,0:T(4,128)S(1)}, s32[4,4,128]{2,1,0:T(4,128)S(1)}, u32[]{:S(2)}, u32[]{:S(2)}) collective-permute-start(s32[4,4,128]{2,1,0:T(4,128)S(1)} %constant_dynamic-update-slice_fusion), channel_id=1, source_target_pairs={{2,0},{3,1},{0,2},{1,3},{6,4},{7,5},{4,6},{5,7},{10,8},{11,9},{8,1... | collective-permute-start | bytes 24584 | tf_op jit(solution)/shard_map/ppermute | solution.py:413
  28.2 2.7 %collective-permute-done.6 = s32[4,4,128]{2,1,0:T(4,128)S(1)} collective-permute-done((s32[4,4,128]{2,1,0:T(4,128)S(1)}, s32[4,4,128]{2,1,0:T(4,128)S(1)}, u32[]{:S(2)}, u32[]{:S(2)}) %collective-permute-start.6) | collective-permute-done | bytes 8224 | tf_op jit(solution)/shard_map/ppermute | solution.py:413
  30.9 1.5 %collective-permute-done.7 = s32[4,4,128]{2,1,0:T(4,128)S(1)} collective-permute-done((s32[4,4,128]{2,1,0:T(4,128)S(1)}, s32[4,4,128]{2,1,0:T(4,128)S(1)}, u32[]{:S(2)}, u32[]{:S(2)}) %collective-permute-start.7) | collective-permute-done | bytes 8224 | tf_op jit(solution)/shard_map/ppermute | solution.py:413
  32.4 0.0 collective-permute-done.8
  32.5 0.1 collective-permute-start.9
  32.6 1.2 %collective-permute-done.9 = s32[4,4,4,128]{3,2,1,0:T(4,128)S(1)} collective-permute-done((s32[4,4,4,128]{3,2,1,0:T(4,128)S(1)}, s32[4,4,4,128]{3,2,1,0:T(4,128)S(1)}, u32[]{:S(2)}, u32[]{:S(2)}) %collective-permute-start.9) | collective-permute-done | bytes 32800 | tf_op jit(solution)/shard_map/ppermute | solution.py:413
  33.7 2.9 %plan.1 = (s32[15]{0:T(128)S(1)}, s32[513]{0:T(1024)S(1)}, s32[513]{0:T(1024)S(1)}, s32[40,128]{1,0:T(8,128)S(1)}, bf16[6,128,128]{2,1,0:T(8,128)(2,1)S(1)}) custom-call(s32[2]{0:T(128)S(1)} %pad_add_fusion.me_ref, s32[128,128]{1,0:T(8,128)S(1)} %bitcast.41), custom_call_target="tpu_custom_call" | custom-call | tf_op jit(solution)/shard_map/plan/pallas_call | solution.py:149
  36.6 21.3 %collective-permute-done.10.rest_1_ = f32[16,128,128]{2,1,0:T(8,128)S(1)} collective-permute-done((f32[16,128,128]{2,1,0:T(8,128)}, f32[16,128,128]{2,1,0:T(8,128)S(1)}, u32[]{:S(2)}, u32[]{:S(2)}) %collective-permute-start.10) | collective-permute-done | bytes 1048608 | tf_op jit(solution)/shard_map/ppermute | solution.py:400
  58.0 0.9 pack.1
  58.8 3.9 %collective-permute-start.11 = (f32[5,128,128]{2,1,0:T(8,128)S(1)}, f32[5,128,128]{2,1,0:T(8,128)S(1)}, u32[]{:S(2)}, u32[]{:S(2)}) collective-permute-start(f32[5,128,128]{2,1,0:T(8,128)S(1)} %get-tuple-element.53), channel_id=1, source_target_pairs={{0,96},{16,112},{32,0},{48,16},{64,32},{80,48},{96,64},{112,80},{1... | collective-permute-start | bytes 983048 | tf_op jit(solution)/shard_map/ppermute | solution.py:400
  62.7 0.3 collective-permute-start.12
  63.0 1.2 %collective-permute-start.13 = (f32[5,128,128]{2,1,0:T(8,128)S(1)}, f32[5,128,128]{2,1,0:T(8,128)S(1)}, u32[]{:S(2)}, u32[]{:S(2)}) collective-permute-start(f32[5,128,128]{2,1,0:T(8,128)S(1)} %get-tuple-element.55), channel_id=1, source_target_pairs={{0,32},{16,48},{32,64},{48,80},{64,96},{80,112},{96,0},{112,16},{1... | collective-permute-start | bytes 983048 | tf_op jit(solution)/shard_map/ppermute | solution.py:400
  64.3 1.7 %overflow.1 = s32[1]{0:T(128)} custom-call(s32[128,128]{1,0:T(8,128)S(1)} %bitcast.42, bf16[6,128,128]{2,1,0:T(8,128)(2,1)S(1)} %get-tuple-element.57.maps_ref), custom_call_target="tpu_custom_call" | custom-call | flops 1000000000 | bytes 100000 | tf_op jit(solution)/shard_map/overflow/pallas_call | solution.py:219
  66.0 0.0 all-gather.4.cloned.1.call-done
  66.0 0.0 copy-start.1
  66.1 2.4 %products.3.rest_3_ = f32[16,128,128]{2,1,0:T(8,128)S(1)} custom-call(s32[513]{0:T(1024)S(1)} %get-tuple-element.56.list_ref, f32[64,128,128]{2,1,0:T(8,128)} %bitcast.43, f32[16,128,128]{2,1,0:T(8,128)} %bitcast.48, f32[16,128,128]{2,1,0:T(8,128)S(1)} %collective-permute-done.10.rest_1_), custom_call_target="tpu_custom_call" | custom-call | flops 100663296 | bytes 1572864 | tf_op jit(solution)/shard_map/products/pallas_call | solution.py:373
  68.5 2.3 %collective-permute-done.11.rest_0_ = f32[5,128,128]{2,1,0:T(8,128)S(1)} collective-permute-done((f32[5,128,128]{2,1,0:T(8,128)S(1)}, f32[5,128,128]{2,1,0:T(8,128)S(1)}, u32[]{:S(2)}, u32[]{:S(2)}) %collective-permute-start.11) | collective-permute-done | bytes 327712 | tf_op jit(solution)/shard_map/ppermute | solution.py:400
  70.8 0.6 collective-permute-done.12.rest_1_
  71.4 3.4 %collective-permute-done.13.rest_2_ = f32[5,128,128]{2,1,0:T(8,128)S(1)} collective-permute-done((f32[5,128,128]{2,1,0:T(8,128)S(1)}, f32[5,128,128]{2,1,0:T(8,128)S(1)}, u32[]{:S(2)}, u32[]{:S(2)}) %collective-permute-start.13) | collective-permute-done | bytes 327712 | tf_op jit(solution)/shard_map/ppermute | solution.py:400
  74.8 0.0 copy-done.1
  74.8 3.9 %products.4 = f32[16,128,128]{2,1,0:T(8,128)S(1)} custom-call(s32[513]{0:T(1024)S(1)} %get-tuple-element.51.list_ref, f32[64,128,128]{2,1,0:T(8,128)S(1)} %bitcast.45, f32[5,128,128]{2,1,0:T(8,128)S(1)} %collective-permute-done.11.rest_0_, f32[5,128,128]{2,1,0:T(8,128)S(1)} %collective-permute-done.12.rest_1_, ...), custom_call_target="tpu_custom_call", output_to_operand_aliasing={{}: (5, {})} | custom-call | flops 100663296 | bytes 1572864 | tf_op jit(solution)/shard_map/products/pallas_call | solution.py:373
  78.7 0.0 copy-start.2
  78.7 1.0 %copy-done.2 = f32[16,128,128]{2,1,0:T(8,128)} copy-done((f32[16,128,128]{2,1,0:T(8,128)}, f32[16,128,128]{2,1,0:T(8,128)S(1)}, u32[]{:S(2)}) %copy-start.2) | copy-done | bytes 1048600
  79.7 0.6 while.10
  (20 shorter events, 0.2 us)
Async XLA Ops:
  6.5 59.5 %all-gather.4.cloned.1.call-start = ((), (), s32[]{:S(2)}) async-start(), calls=%async_computation | async-start | bytes 4456448 | tf_op jit(solution)/shard_map/all_gather | solution.py:430
  8.8 5.1 %collective-permute-start.1 = (s32[128]{0:T(128)S(1)}, s32[128]{0:T(128)S(1)}, u32[]{:S(2)}, u32[]{:S(2)}) collective-permute-start(s32[128]{0:T(128)S(1)} %get-tuple-element.74), channel_id=1, source_target_pairs={{16,0},{17,1},{18,2},{19,3},{20,4},{21,5},{22,6},{23,7},{24,8},{25... | collective-permute-start | bytes 1544 | tf_op jit(solution)/shard_map/ppermute | solution.py:413
  9.2 4.4 %collective-permute-start = (s32[128]{0:T(128)S(1)}, s32[128]{0:T(128)S(1)}, u32[]{:S(2)}, u32[]{:S(2)}) collective-permute-start(s32[128]{0:T(128)S(1)} %get-tuple-element.74), channel_id=1, source_target_pairs={{8,0},{9,1},{10,2},{11,3},{12,4},{13,5},{14,6},{15,7},{0,8},{1,9},... | collective-permute-start | bytes 1544 | tf_op jit(solution)/shard_map/ppermute | solution.py:413
  11.4 3.5 %collective-permute-start.2 = (s32[128]{0:T(128)S(1)}, s32[128]{0:T(128)S(1)}, u32[]{:S(2)}, u32[]{:S(2)}) collective-permute-start(s32[128]{0:T(128)S(1)} %get-tuple-element.74), channel_id=1, source_target_pairs={{24,0},{25,1},{26,2},{27,3},{28,4},{29,5},{30,6},{31,7},{16,8},{17... | collective-permute-start | bytes 1544 | tf_op jit(solution)/shard_map/ppermute | solution.py:413
  12.9 45.1 %collective-permute-start.10 = (f32[16,128,128]{2,1,0:T(8,128)}, f32[16,128,128]{2,1,0:T(8,128)S(1)}, u32[]{:S(2)}, u32[]{:S(2)}) collective-permute-start(f32[16,128,128]{2,1,0:T(8,128)} %bitcast.46), channel_id=1, source_target_pairs={{0,16},{16,0},{32,48},{48,32},{64,80},{80,64},{96,112},{112,96},{1... | collective-permute-start | bytes 3145736 | tf_op jit(solution)/shard_map/ppermute | solution.py:400
  15.0 8.2 %collective-permute-start.5 = (s32[4,128]{1,0:T(4,128)S(1)}, s32[4,128]{1,0:T(4,128)S(1)}, u32[]{:S(2)}, u32[]{:S(2)}) collective-permute-start(s32[4,128]{1,0:T(4,128)S(1)} %dynamic_update_slice.49), channel_id=1, source_target_pairs={{96,0},{97,1},{98,2},{99,3},{100,4},{101,5},{102,6},{103,7},{104,8... | collective-permute-start | bytes 6152 | tf_op jit(solution)/shard_map/ppermute | solution.py:413
  18.1 5.1 %collective-permute-start.4 = (s32[4,128]{1,0:T(4,128)S(1)}, s32[4,128]{1,0:T(4,128)S(1)}, u32[]{:S(2)}, u32[]{:S(2)}) collective-permute-start(s32[4,128]{1,0:T(4,128)S(1)} %dynamic_update_slice.49), channel_id=1, source_target_pairs={{64,0},{65,1},{66,2},{67,3},{68,4},{69,5},{70,6},{71,7},{72,8},{73... | collective-permute-start | bytes 6152 | tf_op jit(solution)/shard_map/ppermute | solution.py:413
  18.7 3.6 %collective-permute-start.3 = (s32[4,128]{1,0:T(4,128)S(1)}, s32[4,128]{1,0:T(4,128)S(1)}, u32[]{:S(2)}, u32[]{:S(2)}) collective-permute-start(s32[4,128]{1,0:T(4,128)S(1)} %dynamic_update_slice.49), channel_id=1, source_target_pairs={{32,0},{33,1},{34,2},{35,3},{36,4},{37,5},{38,6},{39,7},{40,8},{41... | collective-permute-start | bytes 6152 | tf_op jit(solution)/shard_map/ppermute | solution.py:413
  23.2 9.3 %collective-permute-start.8 = (s32[4,4,128]{2,1,0:T(4,128)S(1)}, s32[4,4,128]{2,1,0:T(4,128)S(1)}, u32[]{:S(2)}, u32[]{:S(2)}) collective-permute-start(s32[4,4,128]{2,1,0:T(4,128)S(1)} %constant_dynamic-update-slice_fusion), channel_id=1, source_target_pairs={{6,0},{7,1},{4,2},{5,3},{2,4},{3,5},{0,6},{1,7},{14,8},{15,9},{12,... | collective-permute-start | bytes 24584 | tf_op jit(solution)/shard_map/ppermute | solution.py:413
  27.3 5.2 %collective-permute-start.7 = (s32[4,4,128]{2,1,0:T(4,128)S(1)}, s32[4,4,128]{2,1,0:T(4,128)S(1)}, u32[]{:S(2)}, u32[]{:S(2)}) collective-permute-start(s32[4,4,128]{2,1,0:T(4,128)S(1)} %constant_dynamic-update-slice_fusion), channel_id=1, source_target_pairs={{4,0},{5,1},{6,2},{7,3},{0,4},{1,5},{2,6},{3,7},{12,8},{13,9},{14,... | collective-permute-start | bytes 24584 | tf_op jit(solution)/shard_map/ppermute | solution.py:413
  27.3 3.7 %collective-permute-start.6 = (s32[4,4,128]{2,1,0:T(4,128)S(1)}, s32[4,4,128]{2,1,0:T(4,128)S(1)}, u32[]{:S(2)}, u32[]{:S(2)}) collective-permute-start(s32[4,4,128]{2,1,0:T(4,128)S(1)} %constant_dynamic-update-slice_fusion), channel_id=1, source_target_pairs={{2,0},{3,1},{0,2},{1,3},{6,4},{7,5},{4,6},{5,7},{10,8},{11,9},{8,1... | collective-permute-start | bytes 24584 | tf_op jit(solution)/shard_map/ppermute | solution.py:413
  32.5 1.3 %collective-permute-start.9 = (s32[4,4,4,128]{3,2,1,0:T(4,128)S(1)}, s32[4,4,4,128]{3,2,1,0:T(4,128)S(1)}, u32[]{:S(2)}, u32[]{:S(2)}) collective-permute-start(s32[4,4,4,128]{3,2,1,0:T(4,128)S(1)} %bitcast_dynamic-update-slice_fusion.2), channel_id=1, source_target_pairs={{1,0},{0,1},{3,2},{2,3},{5,4},{4,5},{7,6},{6,7},{9,8},{8,9},{11,10... | collective-permute-start | bytes 98312 | tf_op jit(solution)/shard_map/ppermute | solution.py:413
  58.8 12.0 %collective-permute-start.11 = (f32[5,128,128]{2,1,0:T(8,128)S(1)}, f32[5,128,128]{2,1,0:T(8,128)S(1)}, u32[]{:S(2)}, u32[]{:S(2)}) collective-permute-start(f32[5,128,128]{2,1,0:T(8,128)S(1)} %get-tuple-element.53), channel_id=1, source_target_pairs={{0,96},{16,112},{32,0},{48,16},{64,32},{80,48},{96,64},{112,80},{1... | collective-permute-start | bytes 983048 | tf_op jit(solution)/shard_map/ppermute | solution.py:400
  62.7 8.7 %collective-permute-start.12 = (f32[5,128,128]{2,1,0:T(8,128)S(1)}, f32[5,128,128]{2,1,0:T(8,128)S(1)}, u32[]{:S(2)}, u32[]{:S(2)}) collective-permute-start(f32[5,128,128]{2,1,0:T(8,128)S(1)} %get-tuple-element.54), channel_id=1, source_target_pairs={{0,64},{16,80},{32,96},{48,112},{64,0},{80,16},{96,32},{112,48},{1... | collective-permute-start | bytes 983048 | tf_op jit(solution)/shard_map/ppermute | solution.py:400
  63.0 11.8 %collective-permute-start.13 = (f32[5,128,128]{2,1,0:T(8,128)S(1)}, f32[5,128,128]{2,1,0:T(8,128)S(1)}, u32[]{:S(2)}, u32[]{:S(2)}) collective-permute-start(f32[5,128,128]{2,1,0:T(8,128)S(1)} %get-tuple-element.55), channel_id=1, source_target_pairs={{0,32},{16,48},{32,64},{48,80},{64,96},{80,112},{96,0},{112,16},{1... | collective-permute-start | bytes 983048 | tf_op jit(solution)/shard_map/ppermute | solution.py:400
  66.0 8.8 %copy-start.1 = (f32[16,1,4,128,128]{4,3,2,1,0:T(8,128)S(1)}, f32[16,1,4,128,128]{4,3,2,1,0:T(8,128)}, u32[]{:S(2)}) copy-start(f32[16,1,4,128,128]{4,3,2,1,0:T(8,128)} %all-gather.4.cloned.1.call-done) | copy-start | bytes 12582916
  78.7 1.0 %copy-start.2 = (f32[16,128,128]{2,1,0:T(8,128)}, f32[16,128,128]{2,1,0:T(8,128)S(1)}, u32[]{:S(2)}) copy-start(f32[16,128,128]{2,1,0:T(8,128)S(1)} %products.4) | copy-start | bytes 3145732
Sparse Core Ops, SparseCore 0:
  9.1 49.8 all-gather.3

commit v3 on v1

--- a/solution.py
+++ b/solution.py
@@ -14,6 +14,7 @@
 NEAR = 6
 FAR = 3
 COL = ("x_lo", "z", "core")
+A_PARTS = 10
 LIST = 512
 AHEAD = 8
 
@@ -63,6 +64,11 @@
 
 def c_of(word):
     return word & 15
+
+
+def fetch_a(word, a_refs, dst, sem):
+    a = a_of(word)
+    fetch_block(a >> 3, a & 7, a_refs, dst, sem)
 
 
 def fetch_block(part, at, refs, dst, sem):
@@ -142,7 +148,7 @@
     info_ref[8:16] = b
     info_ref[16:32] = c
     info_ref[32:40] = order
-    here, sent, _ = entries_of(info_ref, row)
+    here, sent, _ = entries_of(info_ref, me_ref)
     extract(here, own_list)
     extract(sent, sent_list)
 
@@ -256,7 +262,8 @@
     list_ref[LIST] = n
 
 
-def entries_of(info_ref, row):
+def entries_of(info_ref, me_ref):
+    row, column = me_ref[0], me_ref[1]
     b, c, order = info_ref[8:16], info_ref[16:32], info_ref[32:40]
     r, p, owner, way = lane_facts(b.shape)
     t = lax.broadcasted_iota(jnp.int32, b.shape, 0)
@@ -264,6 +271,10 @@
     steps = ((owner >> 1) - (row >> 1)) & 3
     part = jnp.where(steps == 0, 0, jnp.where(steps == 3, 1, 2))
     sent = (way > 0) & (rank < jnp.where(way == 1, NEAR, FAR))
+    along = ((p >> 1) - (column >> 1)) & 3
+    beside = ((p ^ column) >> 3) & 1
+    a_part = jnp.where(along == 0, 0, jnp.where(along == 3, 1, jnp.where(along == 1, 2, 3 + beside)))
+    a_at = (a_part + 5 * ((p ^ column) & 1)) * 8 + jnp.where(along == 2, 0, beside * SA)
     found = [[], [], []]
     for s in range(SA):
         lands = lands_at(info_ref[s : s + 1], b)
@@ -271,23 +282,23 @@
         for n in range(c.shape[0]):
             c_slot = jnp.where(lands == c[n : n + 1], n, c_slot)
         live = (c_slot >= 0) & (r == row)
-        a_slot = p * SA + s
+        a_slot = a_at + s
         for found_in, mine, code_of in (
             (found[0], way == 0, code(a_slot, part, (p & 1) * 8 + t, c_slot)),
             (found[1], sent, code(a_slot, (way - 1) & 3, rank, c_slot)),
-            (found[2], (way > 0) & ~sent, code(a_slot, 0, p * 8 + t, c_slot)),
+            (found[2], (way > 0) & ~sent, code(a_slot, owner ^ row, (p & 1) * 8 + t, c_slot)),
         ):
             found_in.append(jnp.where(live & mine, code_of, -1).astype(jnp.float32))
     return [jnp.concatenate(x) for x in found]
 
 
-def multiply_listed(list_ref, a_ref, b_refs, out_ref, a_buf, b_buf, a_sem, b_sem, meanwhile):
+def multiply_listed(list_ref, a_refs, b_refs, out_ref, a_buf, b_buf, a_sem, b_sem, meanwhile):
     count = list_ref[LIST]
 
     def fetch(n):
         slot = n % AHEAD
         word = list_ref[n]
-        pltpu.make_async_copy(a_ref.at[a_of(word)], a_buf.at[slot], a_sem.at[slot]).start()
+        fetch_a(word, a_refs, a_buf.at[slot], a_sem.at[slot])
         fetch_block(part_of(word), at_of(word), b_refs, b_buf.at[slot], b_sem.at[slot])
 
     for n in range(AHEAD):
@@ -300,7 +311,7 @@
 
     def step(n, carry):
         slot = n % AHEAD
-        pltpu.make_async_copy(a_ref.at[0], a_buf.at[slot], a_sem.at[slot]).wait()
+        pltpu.make_async_copy(a_refs[0].at[0], a_buf.at[slot], a_sem.at[slot]).wait()
         pltpu.make_async_copy(b_refs[0].at[0], b_buf.at[slot], b_sem.at[slot]).wait()
         out_ref[c_of(list_ref[n])] += block_product(a_buf[slot], b_buf[slot])
 
@@ -313,42 +324,46 @@
     lax.fori_loop(0, count, step, 0)
 
 
-def own_kernel(list_ref, a_ref, *rest):
-    b_refs, (out_ref, *buffers) = rest[:3], rest[3:]
+def own_kernel(parts, list_ref, *rest):
+    a_refs, b_refs, (out_ref, *buffers) = rest[:A_PARTS], rest[A_PARTS:parts], rest[parts:]
 
     def meanwhile():
         out_ref[...] = jnp.zeros_like(out_ref)
 
-    multiply_listed(list_ref, a_ref, b_refs, out_ref, *buffers, meanwhile)
-
-
-def sent_kernel(list_ref, a_ref, *rest):
-    b_refs, (total_ref, out_ref, *buffers) = rest[:-6], rest[-6:]
+    multiply_listed(list_ref, a_refs, b_refs, out_ref, *buffers, meanwhile)
+
+
+def sent_kernel(parts, list_ref, *rest):
+    a_refs, b_refs = rest[:A_PARTS], rest[A_PARTS:parts]
+    total_ref, out_ref, *buffers = rest[parts:]
 
     def meanwhile():
         out_ref[...] = total_ref[...]
 
-    multiply_listed(list_ref, a_ref, b_refs, out_ref, *buffers, meanwhile)
-
-
-def rest_kernel(me_ref, info_ref, a_ref, b_ref, total_ref, out_ref, rest_list, *buffers):
-    extract(entries_of(info_ref, me_ref[0])[2], rest_list)
+    multiply_listed(list_ref, a_refs, b_refs, out_ref, *buffers, meanwhile)
+
+
+def rest_kernel(parts, me_ref, info_ref, *rest):
+    a_refs, b_refs = rest[:A_PARTS], rest[A_PARTS:parts]
+    total_ref, out_ref, rest_list, *buffers = rest[parts:]
+    extract(entries_of(info_ref, me_ref)[2], rest_list)
 
     def meanwhile():
         out_ref[...] = total_ref[...]
 
-    multiply_listed(rest_list, a_ref, [b_ref], out_ref, *buffers, meanwhile)
-
-
-def products(kernel, leading, a_all, b_parts, total, slots, own_list=False):
-    size = a_all.shape[-1]
+    multiply_listed(rest_list, a_refs, b_refs, out_ref, *buffers, meanwhile)
+
+
+def products(kernel, leading, a_parts, b_parts, total, slots, own_list=False):
+    size = a_parts[0].shape[-1]
+    parts = len(a_parts) + len(b_parts)
     smem = pl.BlockSpec(memory_space=pltpu.SMEM)
     vmem = pl.BlockSpec(memory_space=pltpu.VMEM)
-    operands = [*leading, a_all, *b_parts] + ([] if total is None else [total])
+    operands = [*leading, *a_parts, *b_parts] + ([] if total is None else [total])
     return pl.pallas_call(
-        kernel,
+        functools.partial(kernel, parts),
         in_specs=[smem if x.ndim == 1 else vmem for x in leading]
-        + [pl.BlockSpec(memory_space=pl.ANY)] * (1 + len(b_parts))
+        + [pl.BlockSpec(memory_space=pl.ANY)] * parts
         + ([] if total is None else [vmem]),
         out_specs=vmem,
         out_shape=jax.ShapeDtypeStruct((slots, size, size), jnp.float32),
@@ -372,6 +387,23 @@
     return lax.ppermute(block, "row", [(i, there(i)) for i in range(rows)])
 
 
+def tiles(tile, columns):
+    def moved(block, there):
+        return lax.ppermute(block, COL, [(i, there(i)) for i in range(columns)])
+
+    def on(i):
+        return (i & 9) | ((i + 2) & 6)
+
+    def back(i):
+        return (i & 9) | ((i - 2) & 6)
+
+    n = tile.shape[0]
+    pair = jnp.concatenate([tile, moved(tile, lambda i: i ^ 8)])
+    behind, ahead = moved(pair, on), moved(pair, back)
+    mine = [pair, behind, ahead, moved(behind[:n], on), moved(ahead[n:], back)]
+    return mine + [moved(block, lambda i: i ^ 1) for block in mine]
+
+
 def everywhere(mine, rows, columns):
     axes = ("row", *COL)
     me = lax.axis_index("row") * columns + lax.axis_index(COL)
@@ -399,7 +431,7 @@
     held = hold * sb
     size = a_blocks.shape[-1]
 
-    a_all = lax.all_gather(a_blocks[0, 0], COL).reshape(columns * sa, size, size)
+    a_parts = tiles(a_blocks[0, 0], columns)
 
     own = b_blocks[0, 0].reshape(held, size, size)
     behind = to_row(own, rows, lambda i: (i + 2) % rows)
@@ -421,15 +453,18 @@
         to_row(block, rows, there) for block, (*_, there) in zip(packed, sends)
     ]
 
-    total = products(own_kernel, [own_list], a_all, near, None, sc)
-    total = products(sent_kernel, [sent_list], a_all, [cross, far_own, far_other], total, sc)
+    total = products(own_kernel, [own_list], a_parts, near, None, sc)
+    total = products(
+        sent_kernel, [sent_list], a_parts, [cross, far_own, far_other], total, sc
+    )
 
     trips = overflow(spots, maps)[0]
 
     def trip(state):
         done, total = state
-        whole = lax.all_gather(own, "row").reshape(rows * held, size, size)
-        rest = products(rest_kernel, [me, info], a_all, [whole], total, sc, own_list=True)
+        sent = jnp.where(done >= 0, own, 0)
+        whole = [own] + [to_row(sent, rows, lambda i, n=n: i ^ n) for n in range(1, rows)]
+        rest = products(rest_kernel, [me, info], a_parts, whole, total, sc, own_list=True)
         return done + 1, rest
 
     _, total = lax.while_loop(lambda state: state[0] < trips, trip, (jnp.int32(0), total))

time: 72.6 us -> 76.4 us (1.052); the launches traced: 73 us -> 76 us
  between operations: 13.5 us -> 0.35 us
  starting transfers between devices: 23.1 us -> 35.7 us
  local copies, waits for them, and re-layouts: 1.97 us -> 5.72 us
  Pallas kernels: 11.3 us -> 8.66 us
  waiting for transfers between devices: 21.8 us -> 23.1 us
  other arithmetic: 0.82 us -> 1.66 us
    ppermute x0 -> x10, starting transfers between devices: none -> 9.95 us  [moved(): return lax.ppermute(block, COL, [(i, there(i)) for i in range(columns)])]
    ppermute x0 -> x10, waiting for transfers between devices: none -> 5.63 us  [moved(): return lax.ppermute(block, COL, [(i, there(i)) for i in range(columns)])]
    all_gather x1 -> x0, waiting for transfers between devices: 3.93 us -> none  [per_device(): lax.all_gather(a_blocks[0, 0], COL).reshape(columns * sa, size, size)]
    ppermute x10, starting transfers between devices: 17.7 us -> 19.8 us  [everywhere(): lax.ppermute(held, axes, [(i ^ flip, i) for i in range(rows * columns)])]
    slice x0 -> x2, local copies, waits for them, and re-layouts: none -> 1.94 us  [tiles(): mine = [pair, behind, ahead, moved(behind[:n], on), moved(ahead[n:], back)]]
    ppermute x10, waiting for transfers between devices: 8.03 us -> 9.95 us  [everywhere(): lax.ppermute(held, axes, [(i ^ flip, i) for i in range(rows * columns)])]
    unnamed x4 -> x16, local copies, waits for them, and re-layouts: 0.97 us -> 2.74 us
    pallas_call x2, Pallas kernels: 4.56 us -> 2.97 us  [products(): pl.pallas_call(functools.partial(kernel, parts), in_specs=[smem if x.ndim...]
  transfers between devices with their start and end apart: 16 -> 25, of which waited for: 8 -> 8; matrix products, arithmetic and copies ran while one was open for 2% -> 4% of each run, Pallas kernels for 12% -> 9%
where the time goes in v3:
time: 76.4 us; the launch traced here: 76 us
  starting transfers between devices  35.7 us (47%)
  waiting for transfers between devices  23.1 us (30%)
  Pallas kernels  8.66 us (11%)
  local copies, waits for them, and re-layouts  5.72 us (7%)
  other arithmetic  1.66 us (2%)
  loops' own time  0.82 us (1%)
    ppermute x10, starting transfers between devices, everywhere(): lax.ppermute(held, axes, [(i ^ flip, i) for i in range(rows * columns)])  19.8 us
    ppermute x10, waiting for transfers between devices, everywhere(): lax.ppermute(held, axes, [(i ^ flip, i) for i in range(rows * columns)])  9.95 us
    ppermute x10, starting transfers between devices, moved(): return lax.ppermute(block, COL, [(i, there(i)) for i in range(columns)])  9.95 us
    ppermute x5, waiting for transfers between devices, to_row(): return lax.ppermute(block, 'row', [(i, there(i)) for i in range(rows)])  7.56 us
    ppermute x5, starting transfers between devices, to_row(): return lax.ppermute(block, 'row', [(i, there(i)) for i in range(rows)])  5.95 us
    ppermute x10, waiting for transfers between devices, moved(): return lax.ppermute(block, COL, [(i, there(i)) for i in range(columns)])  5.63 us
    pallas_call x2, Pallas kernels, products(): pl.pallas_call(functools.partial(kernel, parts), in_specs=[smem if x.ndim...  2.97 us
    unnamed x16, local copies, waits for them, and re-layouts  2.74 us
  transfers between devices with their start and end apart: 25, of which 8 were waited for; matrix products, arithmetic and copies ran while one was open for 4% of the time, Pallas kernels for 9%

profile of v3, /device:TPU:1, one launch (start us, length us, event | category | flops | bytes accessed | tf_op | source)
XLA Modules:
  0.0 76.0 jit_solution(9563448513080792923)
XLA Ops:
  0.0 0.8 %reshape_squeeze.6 = s32[16]{0:T(128)S(1)} reshape(s32[1,1,2,8]{3,2,1,0:T(2,128)} %param.10) | data formatting | bytes 128 | tf_op jit(solution)/shard_map/reshape;squeeze | solution.py:442
  0.8 0.7 pad_add_fusion.1
  1.6 3.8 %collective-permute-start.8 = (s32[128]{0:T(128)S(1)}, s32[128]{0:T(128)S(1)}, u32[]{:S(2)}, u32[]{:S(2)}) collective-permute-start(s32[128]{0:T(128)S(1)} %get-tuple-element.239), channel_id=1, source_target_pairs={{64,0},{65,1},{66,2},{67,3},{68,4},{69,5},{70,6},{71,7},{72,8},{73... | collective-permute-start | bytes 1544 | tf_op jit(solution)/shard_map/ppermute | solution.py:417
  5.3 0.4 collective-permute-start.7
  5.7 0.4 collective-permute-start.9
  6.1 2.3 %collective-permute-start.28 = (f32[16,128,128]{2,1,0:T(8,128)}, f32[16,128,128]{2,1,0:T(8,128)S(1)}, u32[]{:S(2)}, u32[]{:S(2)}) collective-permute-start(f32[16,128,128]{2,1,0:T(8,128)} %bitcast.20.rest_0_.rest_10_), channel_id=1, source_target_pairs={{0,96},{16,112},{32,0},{48,16},{64,32},{80,48},{96,64},{112,80},{1... | collective-permute-start | bytes 3145736 | tf_op jit(solution)/shard_map/ppermute | solution.py:387
  8.5 0.1 collective-permute-start.27
  8.5 0.0 collective-permute-done.7
  8.6 1.3 %collective-permute-start.17 = (f32[4,128,128]{2,1,0:T(8,128)S(1)}, f32[4,128,128]{2,1,0:T(8,128)S(1)}, u32[]{:S(2)}, u32[]{:S(2)}) collective-permute-start(f32[4,128,128]{2,1,0:T(8,128)S(1)} %bitcast.36), channel_id=1, source_target_pairs={{0,8},{1,9},{2,10},{3,11},{4,12},{5,13},{6,14},{7,15},{8,0},{9,1},... | collective-permute-start | bytes 786440 | tf_op jit(solution)/shard_map/ppermute | solution.py:392
  9.9 0.0 collective-permute-done.8
  9.9 0.0 collective-permute-done.9
  9.9 0.7 collective-permute-start.10
  10.7 2.5 %collective-permute-start.11 = (s32[4,128]{1,0:T(4,128)S(1)}, s32[4,128]{1,0:T(4,128)S(1)}, u32[]{:S(2)}, u32[]{:S(2)}) collective-permute-start(s32[4,128]{1,0:T(4,128)S(1)} %dynamic_update_slice.49), channel_id=1, source_target_pairs={{16,0},{17,1},{18,2},{19,3},{20,4},{21,5},{22,6},{23,7},{24,8},{25... | collective-permute-start | bytes 6152 | tf_op jit(solution)/shard_map/ppermute | solution.py:417
  13.1 1.6 %collective-permute-done.10 = s32[4,128]{1,0:T(4,128)S(1)} collective-permute-done((s32[4,128]{1,0:T(4,128)S(1)}, s32[4,128]{1,0:T(4,128)S(1)}, u32[]{:S(2)}, u32[]{:S(2)}) %collective-permute-start.10) | collective-permute-done | bytes 2080 | tf_op jit(solution)/shard_map/ppermute | solution.py:417
  14.7 2.5 %collective-permute-start.12 = (s32[4,128]{1,0:T(4,128)S(1)}, s32[4,128]{1,0:T(4,128)S(1)}, u32[]{:S(2)}, u32[]{:S(2)}) collective-permute-start(s32[4,128]{1,0:T(4,128)S(1)} %dynamic_update_slice.49), channel_id=1, source_target_pairs={{24,0},{25,1},{26,2},{27,3},{28,4},{29,5},{30,6},{31,7},{16,8},{17... | collective-permute-start | bytes 6152 | tf_op jit(solution)/shard_map/ppermute | solution.py:417
  17.2 0.0 collective-permute-done.11
  17.2 1.5 %collective-permute-done.12 = s32[4,128]{1,0:T(4,128)S(1)} collective-permute-done((s32[4,128]{1,0:T(4,128)S(1)}, s32[4,128]{1,0:T(4,128)S(1)}, u32[]{:S(2)}, u32[]{:S(2)}) %collective-permute-start.12) | collective-permute-done | bytes 2080 | tf_op jit(solution)/shard_map/ppermute | solution.py:417
  18.6 3.6 %collective-permute-start.14 = (s32[4,4,128]{2,1,0:T(4,128)S(1)}, s32[4,4,128]{2,1,0:T(4,128)S(1)}, u32[]{:S(2)}, u32[]{:S(2)}) collective-permute-start(s32[4,4,128]{2,1,0:T(4,128)S(1)} %constant_dynamic-update-slice_fusion), channel_id=1, source_target_pairs={{4,0},{5,1},{6,2},{7,3},{0,4},{1,5},{2,6},{3,7},{12,8},{13,9},{14,... | collective-permute-start | bytes 24584 | tf_op jit(solution)/shard_map/ppermute | solution.py:417
  22.3 0.8 %collective-permute-start.13 = (s32[4,4,128]{2,1,0:T(4,128)S(1)}, s32[4,4,128]{2,1,0:T(4,128)S(1)}, u32[]{:S(2)}, u32[]{:S(2)}) collective-permute-start(s32[4,4,128]{2,1,0:T(4,128)S(1)} %constant_dynamic-update-slice_fusion), channel_id=1, source_target_pairs={{2,0},{3,1},{0,2},{1,3},{6,4},{7,5},{4,6},{5,7},{10,8},{11,9},{8,1... | collective-permute-start | bytes 24584 | tf_op jit(solution)/shard_map/ppermute | solution.py:417
  23.1 0.0 collective-permute-done.17
  23.1 0.8 %pad_maximum_fusion.rest_0_ = f32[8,128,128]{2,1,0:T(8,128)} fusion(f32[4,128,128]{2,1,0:T(8,128)S(1)} %collective-permute-done.17, f32[4,128,128]{2,1,0:T(8,128)S(1)} %bitcast.37), kind=kLoop, calls=%fused_computation.1 | loop fusion | flops 131072 | bytes 1048576 | tf_op jit(solution)/shard_map/concatenate | solution.py:401
  23.9 0.0 collective-permute-start.19
  23.9 1.2 %collective-permute-done.13 = s32[4,4,128]{2,1,0:T(4,128)S(1)} collective-permute-done((s32[4,4,128]{2,1,0:T(4,128)S(1)}, s32[4,4,128]{2,1,0:T(4,128)S(1)}, u32[]{:S(2)}, u32[]{:S(2)}) %collective-permute-start.13) | collective-permute-done | bytes 8224 | tf_op jit(solution)/shard_map/ppermute | solution.py:417
  25.1 0.4 collective-permute-start.15
  25.6 0.0 collective-permute-done.14
  25.6 0.5 collective-permute-start.18
  26.1 5.7 %collective-permute-done.15 = s32[4,4,128]{2,1,0:T(4,128)S(1)} collective-permute-done((s32[4,4,128]{2,1,0:T(4,128)S(1)}, s32[4,4,128]{2,1,0:T(4,128)S(1)}, u32[]{:S(2)}, u32[]{:S(2)}) %collective-permute-start.15) | collective-permute-done | bytes 8224 | tf_op jit(solution)/shard_map/ppermute | solution.py:417
  31.8 4.7 %collective-permute-start.16 = (s32[4,4,4,128]{3,2,1,0:T(4,128)S(1)}, s32[4,4,4,128]{3,2,1,0:T(4,128)S(1)}, u32[]{:S(2)}, u32[]{:S(2)}) collective-permute-start(s32[4,4,4,128]{3,2,1,0:T(4,128)S(1)} %bitcast_dynamic-update-slice_fusion.2), channel_id=1, source_target_pairs={{1,0},{0,1},{3,2},{2,3},{5,4},{4,5},{7,6},{6,7},{9,8},{8,9},{11,10... | collective-permute-start | bytes 98312 | tf_op jit(solution)/shard_map/ppermute | solution.py:417
  36.6 0.0 collective-permute-done.19.rest_2_
  36.6 1.0 %slice.9 = f32[4,128,128]{2,1,0:T(8,128)S(1)} slice(f32[8,128,128]{2,1,0:T(8,128)} %collective-permute-done.19.rest_2_), slice={[4:8], [0:128], [0:128]} | slice | bytes 524288 | tf_op jit(solution)/shard_map/slice | solution.py:403
  37.5 2.3 %collective-permute-start.22 = (f32[8,128,128]{2,1,0:T(8,128)}, f32[8,128,128]{2,1,0:T(8,128)}, u32[]{:S(2)}, u32[]{:S(2)}) collective-permute-start(f32[8,128,128]{2,1,0:T(8,128)} %pad_maximum_fusion.rest_0_), channel_id=1, source_target_pairs={{0,1},{1,0},{2,3},{3,2},{4,5},{5,4},{6,7},{7,6},{8,9},{9,8},{10,11... | collective-permute-start | bytes 1572872 | tf_op jit(solution)/shard_map/ppermute | solution.py:392
  39.8 0.0 collective-permute-done.16
  39.8 1.3 %collective-permute-start.21 = (f32[4,128,128]{2,1,0:T(8,128)S(1)}, f32[4,128,128]{2,1,0:T(8,128)S(1)}, u32[]{:S(2)}, u32[]{:S(2)}) collective-permute-start(f32[4,128,128]{2,1,0:T(8,128)S(1)} %slice.9), channel_id=1, source_target_pairs={{0,6},{1,7},{2,0},{3,1},{4,2},{5,3},{6,4},{7,5},{8,14},{9,15},{10,... | collective-permute-start | bytes 786440 | tf_op jit(solution)/shard_map/ppermute | solution.py:392
  41.1 0.1 pad_add_fusion.me_ref
  41.2 0.0 collective-permute-done.18.rest_1_
  41.2 0.7 collective-permute-start.24
  41.9 1.0 %slice.8 = f32[4,128,128]{2,1,0:T(8,128)S(1)} slice(f32[8,128,128]{2,1,0:T(8,128)} %collective-permute-done.18.rest_1_), slice={[0:4], [0:128], [0:128]} | slice | bytes 524288 | tf_op jit(solution)/shard_map/slice | solution.py:403
  42.9 4.8 %collective-permute-done.21.rest_4_ = f32[4,128,128]{2,1,0:T(8,128)S(1)} collective-permute-done((f32[4,128,128]{2,1,0:T(8,128)S(1)}, f32[4,128,128]{2,1,0:T(8,128)S(1)}, u32[]{:S(2)}, u32[]{:S(2)}) %collective-permute-start.21) | collective-permute-done | bytes 262176 | tf_op jit(solution)/shard_map/ppermute | solution.py:392
  47.7 0.4 collective-permute-start.20
  48.1 0.0 collective-permute-done.28.rest_2_.rest_12_
  48.1 1.5 %collective-permute-start.23 = (f32[8,128,128]{2,1,0:T(8,128)}, f32[8,128,128]{2,1,0:T(8,128)}, u32[]{:S(2)}, u32[]{:S(2)}) collective-permute-start(f32[8,128,128]{2,1,0:T(8,128)} %collective-permute-done.18.rest_1_), channel_id=1, source_target_pairs={{0,1},{1,0},{2,3},{3,2},{4,5},{5,4},{6,7},{7,6},{8,9},{9,8},{10,11... | collective-permute-start | bytes 1572872 | tf_op jit(solution)/shard_map/ppermute | solution.py:392
  49.6 0.0 collective-permute-done.27.rest_1_.rest_11_
  49.6 0.1 collective-permute-start.26
  49.7 2.4 %plan.1 = (s32[12]{0:T(128)S(1)}, s32[513]{0:T(1024)S(1)}, s32[513]{0:T(1024)S(1)}, s32[40,128]{1,0:T(8,128)}, bf16[6,128,128]{2,1,0:T(8,128)(2,1)S(1)}) custom-call(s32[2]{0:T(128)S(1)} %pad_add_fusion.me_ref, s32[128,128]{1,0:T(8,128)S(1)} %bitcast.34), custom_call_target="tpu_custom_call" | custom-call | tf_op jit(solution)/shard_map/plan/pallas_call | solution.py:159
  52.1 1.6 %pack.1 = (f32[3,128,128]{2,1,0:T(8,128)}, f32[3,128,128]{2,1,0:T(8,128)S(1)}, f32[6,128,128]{2,1,0:T(8,128)S(1)}) custom-call(s32[12]{0:T(128)S(1)} %get-tuple-element.199.list_ref, f32[16,128,128]{2,1,0:T(8,128)} %bitcast.20.rest_0_.rest_10_, f32[16,128,128]{2,1,0:T(8,128)S(1)} %collective-permute-done.27.rest_1_.rest_11_, ...), custom_call_target="tpu_custom_call" | custom-call | tf_op jit(solution)/shard_map/pack/pallas_call | solution.py:194
  53.7 0.0 collective-permute-done.22.rest_5_
  53.7 1.3 %collective-permute-start.29 = (f32[6,128,128]{2,1,0:T(8,128)S(1)}, f32[6,128,128]{2,1,0:T(8,128)S(1)}, u32[]{:S(2)}, u32[]{:S(2)}) collective-permute-start(f32[6,128,128]{2,1,0:T(8,128)S(1)} %get-tuple-element.200), channel_id=1, source_target_pairs={{0,16},{16,0},{32,48},{48,32},{64,80},{80,64},{96,112},{112,96},{1... | collective-permute-start | bytes 1179656 | tf_op jit(solution)/shard_map/ppermute | solution.py:387
  55.1 0.9 %collective-permute-done.20.rest_3_ = f32[4,128,128]{2,1,0:T(8,128)} collective-permute-done((f32[4,128,128]{2,1,0:T(8,128)S(1)}, f32[4,128,128]{2,1,0:T(8,128)}, u32[]{:S(2)}, u32[]{:S(2)}) %collective-permute-start.20) | collective-permute-done | bytes 262176 | tf_op jit(solution)/shard_map/ppermute | solution.py:392
  55.9 1.8 %collective-permute-start.25 = (f32[4,128,128]{2,1,0:T(8,128)}, f32[4,128,128]{2,1,0:T(8,128)}, u32[]{:S(2)}, u32[]{:S(2)}) collective-permute-start(f32[4,128,128]{2,1,0:T(8,128)} %collective-permute-done.20.rest_3_), channel_id=1, source_target_pairs={{0,1},{1,0},{2,3},{3,2},{4,5},{5,4},{6,7},{7,6},{8,9},{9,8},{10,11... | collective-permute-start | bytes 786440 | tf_op jit(solution)/shard_map/ppermute | solution.py:392
  57.7 0.0 collective-permute-done.26.rest_9_
  57.7 0.0 collective-permute-start.30
  57.7 0.0 collective-permute-done.24.rest_7_
  57.7 0.8 %copy-done.3 = f32[8,128,128]{2,1,0:T(8,128)} copy-done((f32[8,128,128]{2,1,0:T(8,128)}, f32[8,128,128]{2,1,0:T(8,128)S(1)}, u32[]{:S(2)}) %copy-start.3) | copy-done | bytes 524312
  58.6 2.3 %collective-permute-start.31 = (f32[3,128,128]{2,1,0:T(8,128)S(1)}, f32[3,128,128]{2,1,0:T(8,128)S(1)}, u32[]{:S(2)}, u32[]{:S(2)}) collective-permute-start(f32[3,128,128]{2,1,0:T(8,128)S(1)} %get-tuple-element.202), channel_id=1, source_target_pairs={{0,48},{16,32},{32,80},{48,64},{64,112},{80,96},{96,16},{112,0},{1... | collective-permute-start | bytes 589832 | tf_op jit(solution)/shard_map/ppermute | solution.py:387
  60.8 0.9 %copy-done.1 = bf16[6,128,128]{2,1,0:T(8,128)(2,1)S(1)} copy-done((bf16[6,128,128]{2,1,0:T(8,128)(2,1)S(1)}, bf16[6,128,128]{2,1,0:T(8,128)(2,1)}, u32[]{:S(2)}) %copy-start.1) | copy-done | bytes 196632
  61.7 1.7 %overflow.1 = s32[1]{0:T(128)} custom-call(s32[128,128]{1,0:T(8,128)S(1)} %bitcast.35, bf16[6,128,128]{2,1,0:T(8,128)(2,1)S(1)} %copy-done.1), custom_call_target="tpu_custom_call" | custom-call | flops 1000000000 | bytes 100000 | tf_op jit(solution)/shard_map/overflow/pallas_call | solution.py:229
  63.5 0.0 collective-permute-done.23.rest_6_
  63.5 0.8 %products.6.rest_13_ = f32[16,128,128]{2,1,0:T(8,128)S(1)} custom-call(s32[513]{0:T(1024)S(1)} %get-tuple-element.203.list_ref, f32[8,128,128]{2,1,0:T(8,128)} %pad_maximum_fusion.rest_0_, f32[8,128,128]{2,1,0:T(8,128)} %collective-permute-done.18.rest_1_, f32[8,128,128]{2,1,0:T(8,128)} %collective-permute-done.19.rest_2_, ...), custom_call_target="tpu_custom_call" | custom-call | flops 100663296 | bytes 1572864 | tf_op jit(solution)/shard_map/products/pallas_call | solution.py:363
  64.4 1.3 %collective-permute-done.30.rest_11_ = f32[3,128,128]{2,1,0:T(8,128)S(1)} collective-permute-done((f32[3,128,128]{2,1,0:T(8,128)}, f32[3,128,128]{2,1,0:T(8,128)S(1)}, u32[]{:S(2)}, u32[]{:S(2)}) %collective-permute-start.30) | collective-permute-done | bytes 196640 | tf_op jit(solution)/shard_map/ppermute | solution.py:387
  65.7 6.2 %collective-permute-done.31.rest_12_ = f32[3,128,128]{2,1,0:T(8,128)S(1)} collective-permute-done((f32[3,128,128]{2,1,0:T(8,128)S(1)}, f32[3,128,128]{2,1,0:T(8,128)S(1)}, u32[]{:S(2)}, u32[]{:S(2)}) %collective-permute-start.31) | collective-permute-done | bytes 196640 | tf_op jit(solution)/shard_map/ppermute | solution.py:387
  71.9 2.1 %products.7 = f32[16,128,128]{2,1,0:T(8,128)S(1)} custom-call(s32[513]{0:T(1024)S(1)} %get-tuple-element.198.list_ref, f32[8,128,128]{2,1,0:T(8,128)} %pad_maximum_fusion.rest_0_, f32[8,128,128]{2,1,0:T(8,128)} %collective-permute-done.18.rest_1_, f32[8,128,128]{2,1,0:T(8,128)} %collective-permute-done.19.rest_2_, ...), custom_call_target="tpu_custom_call", output_to_operand_aliasing={{}: (14, {})} | custom-call | flops 100663296 | bytes 1572864 | tf_op jit(solution)/shard_map/products/pallas_call | solution.py:363
  74.1 0.0 copy-start.2
  74.1 1.0 %copy-done.2 = f32[16,128,128]{2,1,0:T(8,128)} copy-done((f32[16,128,128]{2,1,0:T(8,128)}, f32[16,128,128]{2,1,0:T(8,128)S(1)}, u32[]{:S(2)}) %copy-start.2) | copy-done | bytes 1048600
  75.0 0.8 %while.12 = (s32[]{:T(128)}, f32[16,128,128]{2,1,0:T(8,128)}, s32[]{:T(128)}, f32[16,128,128]{2,1,0:T(8,128)}, s32[2]{0:T(128)S(1)}, /*index=5*/s32[40,128]{1,0:...) while((s32[]{:T(128)}, f32[16,128,128]{2,1,0:T(8,128)}, ...), condition=%wide.region_1.2_spmd, body=%wide.region_0.1_spmd.sunk | while | flops 100925440 | bytes 34161152 | solution.py:470
  (34 shorter events, 0.3 us)
Async XLA Ops:
  0.0 8.6 %copy-start.9 = (f32[1,1,4,128,128]{4,3,2,1,0:T(8,128)S(1)}, f32[1,1,4,128,128]{4,3,2,1,0:T(8,128)}, u32[]{:S(2)}) copy-start(f32[1,1,4,128,128]{4,3,2,1,0:T(8,128)} %param.7) | copy-start | bytes 786436
  1.6 8.3 %collective-permute-start.8 = (s32[128]{0:T(128)S(1)}, s32[128]{0:T(128)S(1)}, u32[]{:S(2)}, u32[]{:S(2)}) collective-permute-start(s32[128]{0:T(128)S(1)} %get-tuple-element.239), channel_id=1, source_target_pairs={{64,0},{65,1},{66,2},{67,3},{68,4},{69,5},{70,6},{71,7},{72,8},{73... | collective-permute-start | bytes 1544 | tf_op jit(solution)/shard_map/ppermute | solution.py:417
  5.3 3.2 %collective-permute-start.7 = (s32[128]{0:T(128)S(1)}, s32[128]{0:T(128)S(1)}, u32[]{:S(2)}, u32[]{:S(2)}) collective-permute-start(s32[128]{0:T(128)S(1)} %get-tuple-element.239), channel_id=1, source_target_pairs={{32,0},{33,1},{34,2},{35,3},{36,4},{37,5},{38,6},{39,7},{40,8},{41... | collective-permute-start | bytes 1544 | tf_op jit(solution)/shard_map/ppermute | solution.py:417
  5.7 4.2 %collective-permute-start.9 = (s32[128]{0:T(128)S(1)}, s32[128]{0:T(128)S(1)}, u32[]{:S(2)}, u32[]{:S(2)}) collective-permute-start(s32[128]{0:T(128)S(1)} %get-tuple-element.239), channel_id=1, source_target_pairs={{96,0},{97,1},{98,2},{99,3},{100,4},{101,5},{102,6},{103,7},{104,8... | collective-permute-start | bytes 1544 | tf_op jit(solution)/shard_map/ppermute | solution.py:417
  6.1 42.0 %collective-permute-start.28 = (f32[16,128,128]{2,1,0:T(8,128)}, f32[16,128,128]{2,1,0:T(8,128)S(1)}, u32[]{:S(2)}, u32[]{:S(2)}) collective-permute-start(f32[16,128,128]{2,1,0:T(8,128)} %bitcast.20.rest_0_.rest_10_), channel_id=1, source_target_pairs={{0,96},{16,112},{32,0},{48,16},{64,32},{80,48},{96,64},{112,80},{1... | collective-permute-start | bytes 3145736 | tf_op jit(solution)/shard_map/ppermute | solution.py:387
  8.5 41.2 %collective-permute-start.27 = (f32[16,128,128]{2,1,0:T(8,128)}, f32[16,128,128]{2,1,0:T(8,128)S(1)}, u32[]{:S(2)}, u32[]{:S(2)}) collective-permute-start(f32[16,128,128]{2,1,0:T(8,128)} %bitcast.20.rest_0_.rest_10_), channel_id=1, source_target_pairs={{0,32},{16,48},{32,64},{48,80},{64,96},{80,112},{96,0},{112,16},{1... | collective-permute-start | bytes 3145736 | tf_op jit(solution)/shard_map/ppermute | solution.py:387
  8.6 14.5 %collective-permute-start.17 = (f32[4,128,128]{2,1,0:T(8,128)S(1)}, f32[4,128,128]{2,1,0:T(8,128)S(1)}, u32[]{:S(2)}, u32[]{:S(2)}) collective-permute-start(f32[4,128,128]{2,1,0:T(8,128)S(1)} %bitcast.36), channel_id=1, source_target_pairs={{0,8},{1,9},{2,10},{3,11},{4,12},{5,13},{6,14},{7,15},{8,0},{9,1},... | collective-permute-start | bytes 786440 | tf_op jit(solution)/shard_map/ppermute | solution.py:392
  9.9 4.8 %collective-permute-start.10 = (s32[4,128]{1,0:T(4,128)S(1)}, s32[4,128]{1,0:T(4,128)S(1)}, u32[]{:S(2)}, u32[]{:S(2)}) collective-permute-start(s32[4,128]{1,0:T(4,128)S(1)} %dynamic_update_slice.49), channel_id=1, source_target_pairs={{8,0},{9,1},{10,2},{11,3},{12,4},{13,5},{14,6},{15,7},{0,8},{1,9},... | collective-permute-start | bytes 6152 | tf_op jit(solution)/shard_map/ppermute | solution.py:417
  10.7 6.5 %collective-permute-start.11 = (s32[4,128]{1,0:T(4,128)S(1)}, s32[4,128]{1,0:T(4,128)S(1)}, u32[]{:S(2)}, u32[]{:S(2)}) collective-permute-start(s32[4,128]{1,0:T(4,128)S(1)} %dynamic_update_slice.49), channel_id=1, source_target_pairs={{16,0},{17,1},{18,2},{19,3},{20,4},{21,5},{22,6},{23,7},{24,8},{25... | collective-permute-start | bytes 6152 | tf_op jit(solution)/shard_map/ppermute | solution.py:417
  14.7 3.9 %collective-permute-start.12 = (s32[4,128]{1,0:T(4,128)S(1)}, s32[4,128]{1,0:T(4,128)S(1)}, u32[]{:S(2)}, u32[]{:S(2)}) collective-permute-start(s32[4,128]{1,0:T(4,128)S(1)} %dynamic_update_slice.49), channel_id=1, source_target_pairs={{24,0},{25,1},{26,2},{27,3},{28,4},{29,5},{30,6},{31,7},{16,8},{17... | collective-permute-start | bytes 6152 | tf_op jit(solution)/shard_map/ppermute | solution.py:417
  18.6 6.9 %collective-permute-start.14 = (s32[4,4,128]{2,1,0:T(4,128)S(1)}, s32[4,4,128]{2,1,0:T(4,128)S(1)}, u32[]{:S(2)}, u32[]{:S(2)}) collective-permute-start(s32[4,4,128]{2,1,0:T(4,128)S(1)} %constant_dynamic-update-slice_fusion), channel_id=1, source_target_pairs={{4,0},{5,1},{6,2},{7,3},{0,4},{1,5},{2,6},{3,7},{12,8},{13,9},{14,... | collective-permute-start | bytes 24584 | tf_op jit(solution)/shard_map/ppermute | solution.py:417
  22.3 2.9 %collective-permute-start.13 = (s32[4,4,128]{2,1,0:T(4,128)S(1)}, s32[4,4,128]{2,1,0:T(4,128)S(1)}, u32[]{:S(2)}, u32[]{:S(2)}) collective-permute-start(s32[4,4,128]{2,1,0:T(4,128)S(1)} %constant_dynamic-update-slice_fusion), channel_id=1, source_target_pairs={{2,0},{3,1},{0,2},{1,3},{6,4},{7,5},{4,6},{5,7},{10,8},{11,9},{8,1... | collective-permute-start | bytes 24584 | tf_op jit(solution)/shard_map/ppermute | solution.py:417
  23.9 12.6 %collective-permute-start.19 = (f32[8,128,128]{2,1,0:T(8,128)}, f32[8,128,128]{2,1,0:T(8,128)}, u32[]{:S(2)}, u32[]{:S(2)}) collective-permute-start(f32[8,128,128]{2,1,0:T(8,128)} %pad_maximum_fusion.rest_0_), channel_id=1, source_target_pairs={{0,6},{1,7},{2,0},{3,1},{4,2},{5,3},{6,4},{7,5},{8,14},{9,15},{10,... | collective-permute-start | bytes 1572872 | tf_op jit(solution)/shard_map/ppermute | solution.py:392
  25.1 6.7 %collective-permute-start.15 = (s32[4,4,128]{2,1,0:T(4,128)S(1)}, s32[4,4,128]{2,1,0:T(4,128)S(1)}, u32[]{:S(2)}, u32[]{:S(2)}) collective-permute-start(s32[4,4,128]{2,1,0:T(4,128)S(1)} %constant_dynamic-update-slice_fusion), channel_id=1, source_target_pairs={{6,0},{7,1},{4,2},{5,3},{2,4},{3,5},{0,6},{1,7},{14,8},{15,9},{12,... | collective-permute-start | bytes 24584 | tf_op jit(solution)/shard_map/ppermute | solution.py:417
  25.6 15.6 %collective-permute-start.18 = (f32[8,128,128]{2,1,0:T(8,128)}, f32[8,128,128]{2,1,0:T(8,128)}, u32[]{:S(2)}, u32[]{:S(2)}) collective-permute-start(f32[8,128,128]{2,1,0:T(8,128)} %pad_maximum_fusion.rest_0_), channel_id=1, source_target_pairs={{0,2},{1,3},{2,4},{3,5},{4,6},{5,7},{6,0},{7,1},{8,10},{9,11},{10,... | collective-permute-start | bytes 1572872 | tf_op jit(solution)/shard_map/ppermute | solution.py:392
  31.8 8.0 %collective-permute-start.16 = (s32[4,4,4,128]{3,2,1,0:T(4,128)S(1)}, s32[4,4,4,128]{3,2,1,0:T(4,128)S(1)}, u32[]{:S(2)}, u32[]{:S(2)}) collective-permute-start(s32[4,4,4,128]{3,2,1,0:T(4,128)S(1)} %bitcast_dynamic-update-slice_fusion.2), channel_id=1, source_target_pairs={{1,0},{0,1},{3,2},{2,3},{5,4},{4,5},{7,6},{6,7},{9,8},{8,9},{11,10... | collective-permute-start | bytes 98312 | tf_op jit(solution)/shard_map/ppermute | solution.py:417
  37.5 16.2 %collective-permute-start.22 = (f32[8,128,128]{2,1,0:T(8,128)}, f32[8,128,128]{2,1,0:T(8,128)}, u32[]{:S(2)}, u32[]{:S(2)}) collective-permute-start(f32[8,128,128]{2,1,0:T(8,128)} %pad_maximum_fusion.rest_0_), channel_id=1, source_target_pairs={{0,1},{1,0},{2,3},{3,2},{4,5},{5,4},{6,7},{7,6},{8,9},{9,8},{10,11... | collective-permute-start | bytes 1572872 | tf_op jit(solution)/shard_map/ppermute | solution.py:392
  39.8 7.9 %collective-permute-start.21 = (f32[4,128,128]{2,1,0:T(8,128)S(1)}, f32[4,128,128]{2,1,0:T(8,128)S(1)}, u32[]{:S(2)}, u32[]{:S(2)}) collective-permute-start(f32[4,128,128]{2,1,0:T(8,128)S(1)} %slice.9), channel_id=1, source_target_pairs={{0,6},{1,7},{2,0},{3,1},{4,2},{5,3},{6,4},{7,5},{8,14},{9,15},{10,... | collective-permute-start | bytes 786440 | tf_op jit(solution)/shard_map/ppermute | solution.py:392
  41.2 16.5 %collective-permute-start.24 = (f32[8,128,128]{2,1,0:T(8,128)}, f32[8,128,128]{2,1,0:T(8,128)S(1)}, u32[]{:S(2)}, u32[]{:S(2)}) collective-permute-start(f32[8,128,128]{2,1,0:T(8,128)} %collective-permute-done.19.rest_2_), channel_id=1, source_target_pairs={{0,1},{1,0},{2,3},{3,2},{4,5},{5,4},{6,7},{7,6},{8,9},{9,8},{10,11... | collective-permute-start | bytes 1572872 | tf_op jit(solution)/shard_map/ppermute | solution.py:392
  47.7 6.1 %copy-start.5 = (f32[4,128,128]{2,1,0:T(8,128)}, f32[4,128,128]{2,1,0:T(8,128)S(1)}, u32[]{:S(2)}) copy-start(f32[4,128,128]{2,1,0:T(8,128)S(1)} %collective-permute-done.21.rest_4_) | copy-start | bytes 786436
  47.7 8.3 %collective-permute-start.20 = (f32[4,128,128]{2,1,0:T(8,128)S(1)}, f32[4,128,128]{2,1,0:T(8,128)}, u32[]{:S(2)}, u32[]{:S(2)}) collective-permute-start(f32[4,128,128]{2,1,0:T(8,128)S(1)} %slice.8), channel_id=1, source_target_pairs={{0,2},{1,3},{2,4},{3,5},{4,6},{5,7},{6,0},{7,1},{8,10},{9,11},{10,... | collective-permute-start | bytes 786440 | tf_op jit(solution)/shard_map/ppermute | solution.py:392
  48.1 15.4 %collective-permute-start.23 = (f32[8,128,128]{2,1,0:T(8,128)}, f32[8,128,128]{2,1,0:T(8,128)}, u32[]{:S(2)}, u32[]{:S(2)}) collective-permute-start(f32[8,128,128]{2,1,0:T(8,128)} %collective-permute-done.18.rest_1_), channel_id=1, source_target_pairs={{0,1},{1,0},{2,3},{3,2},{4,5},{5,4},{6,7},{7,6},{8,9},{9,8},{10,11... | collective-permute-start | bytes 1572872 | tf_op jit(solution)/shard_map/ppermute | solution.py:392
  49.6 8.1 %collective-permute-start.26 = (f32[4,128,128]{2,1,0:T(8,128)S(1)}, f32[4,128,128]{2,1,0:T(8,128)}, u32[]{:S(2)}, u32[]{:S(2)}) collective-permute-start(f32[4,128,128]{2,1,0:T(8,128)S(1)} %collective-permute-done.21.rest_4_), channel_id=1, source_target_pairs={{0,1},{1,0},{2,3},{3,2},{4,5},{5,4},{6,7},{7,6},{8,9},{9,8},{10,11... | collective-permute-start | bytes 786440 | tf_op jit(solution)/shard_map/ppermute | solution.py:392
  52.1 1.6 %copy-start = (bf16[6,128,128]{2,1,0:T(8,128)(2,1)}, bf16[6,128,128]{2,1,0:T(8,128)(2,1)S(1)}, u32[]{:S(2)}) copy-start(bf16[6,128,128]{2,1,0:T(8,128)(2,1)S(1)} %get-tuple-element.204.maps_ref) | copy-start | bytes 589828
  53.7 18.2 %collective-permute-start.29 = (f32[6,128,128]{2,1,0:T(8,128)S(1)}, f32[6,128,128]{2,1,0:T(8,128)S(1)}, u32[]{:S(2)}, u32[]{:S(2)}) collective-permute-start(f32[6,128,128]{2,1,0:T(8,128)S(1)} %get-tuple-element.200), channel_id=1, source_target_pairs={{0,16},{16,0},{32,48},{48,32},{64,80},{80,64},{96,112},{112,96},{1... | collective-permute-start | bytes 1179656 | tf_op jit(solution)/shard_map/ppermute | solution.py:387
  55.9 7.5 %collective-permute-start.25 = (f32[4,128,128]{2,1,0:T(8,128)}, f32[4,128,128]{2,1,0:T(8,128)}, u32[]{:S(2)}, u32[]{:S(2)}) collective-permute-start(f32[4,128,128]{2,1,0:T(8,128)} %collective-permute-done.20.rest_3_), channel_id=1, source_target_pairs={{0,1},{1,0},{2,3},{3,2},{4,5},{5,4},{6,7},{7,6},{8,9},{9,8},{10,11... | collective-permute-start | bytes 786440 | tf_op jit(solution)/shard_map/ppermute | solution.py:392
  57.7 8.0 %collective-permute-start.30 = (f32[3,128,128]{2,1,0:T(8,128)}, f32[3,128,128]{2,1,0:T(8,128)S(1)}, u32[]{:S(2)}, u32[]{:S(2)}) collective-permute-start(f32[3,128,128]{2,1,0:T(8,128)} %get-tuple-element.201), channel_id=1, source_target_pairs={{0,32},{16,48},{32,64},{48,80},{64,96},{80,112},{96,0},{112,16},{1... | collective-permute-start | bytes 589832 | tf_op jit(solution)/shard_map/ppermute | solution.py:387
  57.7 0.8 %copy-start.3 = (f32[8,128,128]{2,1,0:T(8,128)}, f32[8,128,128]{2,1,0:T(8,128)S(1)}, u32[]{:S(2)}) copy-start(f32[8,128,128]{2,1,0:T(8,128)S(1)} %collective-permute-done.24.rest_7_) | copy-start | bytes 1572868
  58.6 13.4 %collective-permute-start.31 = (f32[3,128,128]{2,1,0:T(8,128)S(1)}, f32[3,128,128]{2,1,0:T(8,128)S(1)}, u32[]{:S(2)}, u32[]{:S(2)}) collective-permute-start(f32[3,128,128]{2,1,0:T(8,128)S(1)} %get-tuple-element.202), channel_id=1, source_target_pairs={{0,48},{16,32},{32,80},{48,64},{64,112},{80,96},{96,16},{112,0},{1... | collective-permute-start | bytes 589832 | tf_op jit(solution)/shard_map/ppermute | solution.py:387
  60.8 0.9 %copy-start.1 = (bf16[6,128,128]{2,1,0:T(8,128)(2,1)S(1)}, bf16[6,128,128]{2,1,0:T(8,128)(2,1)}, u32[]{:S(2)}) copy-start(bf16[6,128,128]{2,1,0:T(8,128)(2,1)} %copy-done) | copy-start | bytes 589828
  61.7 1.8 %copy-start.4 = (f32[8,128,128]{2,1,0:T(8,128)S(1)}, f32[8,128,128]{2,1,0:T(8,128)}, u32[]{:S(2)}) copy-start(f32[8,128,128]{2,1,0:T(8,128)} %copy-done.3) | copy-start | bytes 1572868
  61.7 1.8 %copy-start.6 = (f32[4,128,128]{2,1,0:T(8,128)S(1)}, f32[4,128,128]{2,1,0:T(8,128)}, u32[]{:S(2)}) copy-start(f32[4,128,128]{2,1,0:T(8,128)} %copy-done.5) | copy-start | bytes 786436
  74.1 1.0 %copy-start.2 = (f32[16,128,128]{2,1,0:T(8,128)}, f32[16,128,128]{2,1,0:T(8,128)S(1)}, u32[]{:S(2)}) copy-start(f32[16,128,128]{2,1,0:T(8,128)S(1)} %products.7) | copy-start | bytes 3145732
